TPU v7x, 128 devices: a whole 4x4x4 slice. The times are simulated.
128 devices in a mesh: section: 2 (over y_hi), track: 64 (over x, z, y_lo, core).
Axes of the slice: x: 4, y: 4 (y_hi: 2, y_lo: 2; y = y_hi * 2 + y_lo), z: 4, core: 2. Of those that a mesh axis runs over, the one named last changes fastest.
Arguments:
- raw_echoes: bfloat16 [24576, 512], P(('track', 'section')), may hold values from -6 to 6
- first_target: int32 [64], P('track'), may hold values from 0 to 2047, as said below
- aperture_first: int32 [64], P('track'), may hold values from -2 to 62, as said below
- look_start: int32 [256], P('track'), may hold values from 0 to 2047, as said below
Outputs:
- looks: float32 [256, 256], P('track', 'section')
Inputs may be any that keep to these rules, and one draw needn't show every extreme that they name: first_target[j] lies among j * 32 .. j * 32 + 31; the first block's is 0 and the last block's is its largest value. aperture_first[j] is j - 2 or j - 1; the first block's is the former and the last block's the latter. Look l starts inside target block l // 4: look_start[l] lies among (l // 4) * 32 .. (l // 4) * 32 + 31; the first look starts at 0, the last look of the first block at 31, and the last look at 2047.
All inputs are finite; a program needn't handle non-finite values.
Results may differ from a plain program's by a relative error of at most 0.001.
Values may be sent and summed in bfloat16 or wider, within the bound.
No kernel may reach another device: no remote copies, remote signals or barrier semaphores. Data moves between devices by JAX's collectives and lax.ppermute only.
A program may use at most 64 MiB of HBM per device.

v0:
```python
import math

import jax
import jax.numpy as jnp
from jax import lax
from jax.sharding import PartitionSpec as P

ECH_DEV = 384
TB = 32
LOOK = 16
HALF_AP = 2


BLOCK_LENGTH = 1200.0
ALTITUDE = 1300000.0
WAVE_CENTRE = 568.6
WAVE_SPAN = 13.4
CHIRP_RATE = 0.37
HIGHEST = lax.Precision.HIGHEST


def from_behind(value, axis, steps):
    count = lax.axis_size(axis)
    first, last = (max(0, -steps), min(count, count - steps))
    return lax.ppermute(value, axis, [(source, source + steps) for source in range(first, last)])


def chirp_phase(samples):
    position = jnp.arange(samples, dtype=jnp.float32) - float(samples // 2)
    return -math.pi * CHIRP_RATE / samples * position * position


def fourier_parts(samples, first_rows, count_rows, count_cols):
    row_index = jnp.arange(count_rows, dtype=jnp.int32) + first_rows
    col_index = jnp.arange(count_cols, dtype=jnp.int32)
    turns = row_index[:, None] * col_index[None, :] % samples
    angle = turns.astype(jnp.float32) * (2.0 * math.pi / samples)
    factor = 1.0 / math.sqrt(samples)
    return (jnp.cos(angle) * factor, jnp.sin(angle) * factor)


def kernel_sum(signal_real, signal_imag, offset, first_off, wavenumber):
    echo_count = signal_real.shape[0]
    columns = signal_real.shape[1]
    part_rows = math.gcd(echo_count, 256)
    target_place = (
        BLOCK_LENGTH / TB * (first_off + jnp.arange(TB, dtype=jnp.int32)).astype(jnp.float32)
    )

    def add_part(total, part_index):
        start = part_index * part_rows
        rows_real = lax.dynamic_slice_in_dim(signal_real, start, part_rows, 0)
        rows_imag = lax.dynamic_slice_in_dim(signal_imag, start, part_rows, 0)
        echo_index = offset * echo_count + start + jnp.arange(part_rows, dtype=jnp.int32)
        echo_place = BLOCK_LENGTH / ECH_DEV * echo_index.astype(jnp.float32)
        along = echo_place[None, :] - target_place[:, None]
        delay = along * along / (jnp.sqrt(ALTITUDE * ALTITUDE + along * along) + ALTITUDE)
        theta = delay[:, :, None] * wavenumber[None, None, :]
        cos_kernel = jnp.cos(theta)
        sin_kernel = jnp.sin(theta)
        real_part = jnp.einsum("tef,ef->tf", cos_kernel, rows_real) + jnp.einsum(
            "tef,ef->tf", sin_kernel, rows_imag
        )
        imag_part = jnp.einsum("tef,ef->tf", cos_kernel, rows_imag) - jnp.einsum(
            "tef,ef->tf", sin_kernel, rows_real
        )
        return (total + jnp.concatenate([real_part, imag_part], 1), None)

    initial = jnp.zeros((TB, 2 * columns), jnp.float32)
    total, unused = lax.scan(
        add_part, initial, jnp.arange(echo_count // part_rows, dtype=jnp.int32)
    )
    return total


def per_device(raw_echoes, first_target, aperture_first, look_start):
    samples = raw_echoes.shape[1] // 2
    half = samples // 2
    section_index = lax.axis_index("section")
    block_index = lax.axis_index("track")
    raw = raw_echoes.astype(jnp.float32)
    phase = chirp_phase(samples)
    rot_cos = jnp.cos(phase)
    rot_sin = jnp.sin(phase)
    raw_real = raw[:, :samples]
    raw_imag = raw[:, samples:]
    der_real = raw_real * rot_cos - raw_imag * rot_sin
    der_imag = raw_real * rot_sin + raw_imag * rot_cos
    cosine, sine = fourier_parts(samples, 0, samples, samples)
    table_parts = []
    for half_index in range(2):
        cos_part = cosine[:, half_index * half : (half_index + 1) * half]
        sin_part = sine[:, half_index * half : (half_index + 1) * half]
        upper = jnp.concatenate([cos_part, -sin_part], 1)
        lower = jnp.concatenate([sin_part, cos_part], 1)
        table_parts.append(jnp.concatenate([upper, lower], 0))
    compress_table = jnp.concatenate(table_parts, 1)
    compressed = jnp.dot(
        jnp.concatenate([der_real, der_imag], 1), compress_table, precision=HIGHEST
    ).astype(jnp.bfloat16)
    own_block = lax.all_to_all(compressed, "section", split_axis=1, concat_axis=0, tiled=True)
    freq_index = section_index * half + jnp.arange(half, dtype=jnp.int32)
    wavenumber = WAVE_CENTRE + (freq_index.astype(jnp.float32) - float(samples // 2)) * (
        WAVE_SPAN / samples
    )
    own_first = first_target[0] - block_index * TB
    own_lowest = aperture_first[0]

    def contribution(block, offset, first_off, lowest, target_block):
        source = target_block + offset
        inside = (source >= lowest) & (source < lowest + 2 * HALF_AP)
        term = kernel_sum(
            block[:, :half].astype(jnp.float32),
            block[:, half:].astype(jnp.float32),
            offset,
            first_off,
            wavenumber,
        )
        return jnp.where(inside, term, jnp.float32(0.0))

    image = contribution(own_block, 0, own_first, own_lowest, block_index)
    upward = own_block
    downward = own_block
    for hop_count in range(1, HALF_AP + 1):
        upward = from_behind(upward, "track", 1)
        downward = from_behind(downward, "track", -1)
        image = image + contribution(upward, -hop_count, own_first, own_lowest, block_index)
        image = image + contribution(downward, hop_count, own_first, own_lowest, block_index)
    image = image * (1.0 / math.sqrt(2 * HALF_AP * ECH_DEV))
    range_cos, range_sin = fourier_parts(samples, section_index * half, half, samples)
    range_parts = []
    for half_index in range(2):
        cos_part = range_cos[:, half_index * half : (half_index + 1) * half]
        sin_part = range_sin[:, half_index * half : (half_index + 1) * half]
        upper = jnp.concatenate([cos_part, sin_part], 1)
        lower = jnp.concatenate([-sin_part, cos_part], 1)
        range_parts.append(jnp.concatenate([upper, lower], 0))
    range_table = jnp.concatenate(range_parts, 1)
    partial_field = jnp.dot(image, range_table, precision=HIGHEST)
    own_field = lax.psum_scatter(partial_field, "section", scatter_dimension=1, tiled=True)
    power = own_field[:, :half] * own_field[:, :half] + own_field[:, half:] * own_field[:, half:]
    next_rows = from_behind(power[:LOOK], "track", -1)
    extended = jnp.concatenate([power, next_rows], 0)
    local_start = look_start - block_index * TB
    row_place = jnp.arange(TB + LOOK, dtype=jnp.int32)
    window = (
        (row_place[None, :] >= local_start[:, None])
        & (row_place[None, :] < local_start[:, None] + LOOK)
    ).astype(jnp.float32)
    return jnp.dot(window, extended, precision=HIGHEST) / LOOK


def solution(mesh):
    return jax.shard_map(
        per_device,
        mesh=mesh,
        in_specs=(P(("track", "section"), None), P("track"), P("track"), P("track")),
        out_specs=P("track", "section"),
        check_vma=False,
    )
```

profile of v0, /device:TPU:7, one launch (start us, length us, event | category | flops | bytes accessed | tf_op | source)
XLA Modules:
  0.0 230.2 jit_solution(2662342704008240928)
XLA Ops:
  6.5 1.0 cosine_multiply_fusion
  7.5 1.0 sine_multiply_fusion
  8.7 0.9 convolution_convert_fusion
  9.6 0.7 copy.139
  10.3 4.2 %all-to-all-start = ((bf16[192,2,256]{2,0,1:T(8,128)(2,1)}), bf16[192,2,256]{2,0,1:T(8,128)(2,1)S(1)}, u32[]{:S(2)}, u32[]{:S(2)}) async-start(bf16[192,2,256]{2,0,1:T(8,128)(2,1)} %bitcast.173), calls=%async_computation | async-start | bytes 393216 | tf_op jit(solution)/shard_map/all_to_all | solution.py:101
  16.5 3.2 %all-to-all-done = bf16[192,2,256]{2,0,1:T(8,128)(2,1)S(1)} async-done(((bf16[192,2,256]{2,0,1:T(8,128)(2,1)}), bf16[192,2,256]{2,0,1:T(8,128)(2,1)S(1)}, u32[]{:S(2)}, u32[]{:S(2)}) %all-to-all-start) | async-done | bytes 196640 | tf_op jit(solution)/shard_map/all_to_all | solution.py:101
  19.6 4.3 %collective-permute-start = (bf16[384,256]{1,0:T(8,128)(2,1)S(1)}, bf16[384,256]{1,0:T(8,128)(2,1)S(1)}, u32[]{:S(2)}, u32[]{:S(2)}) collective-permute-start(bf16[384,256]{1,0:T(8,128)(2,1)S(1)} %bitcast.231), channel_id=1, source_target_pairs={{0,1},{1,2},{2,3},{3,4},{4,5},{5,6},{6,7},{7,8},{8,9},{9,10},{10,1... | collective-permute-start | bytes 589832 | tf_op jit(solution)/shard_map/ppermute | solution.py:25
  23.9 1.9 collective-permute-start.1
  25.9 33.5 %while.55 = (s32[]{:T(128)}, f32[32,256]{1,0:T(8,128)S(1)}, s32[3]{0:T(128)S(1)}, f32[384,128]{1,0:T(8,128)S(1)}, f32[384,128]{1,0:T(8,128)S(1)}, /*index=5*/s32...) while((s32[]{:T(128)}, f32[32,256]{1,0:T(8,128)S(1)}, ...), condition=%wide.region_1.2_spmd.clone, body=%wide.region_0.1_spmd.clone.sunk | while | flops 4756583 | bytes 690625 | solution.py:70
  25.9 0.7 dynamic_slice.82
  27.4 9.6 %fusion.156 = (f32[128,32]{0,1:T(8,128)S(1)}, f32[128,32]{0,1:T(8,128)S(1)}, f32[128,32]{0,1:T(8,128)S(1)}, f32[128,32]{0,1:T(8,128)S(1)}) fusion(f32[128,128]{0,1:T(8,128)S(1)} %get-tuple-element.706, f32[128]{0:T(128)S(1)} %multiply_add_fusion.11, f32[32,128]{1,0:T(8,128)S(1)} %add_divide_fusion.10, f32[128,128]{0,1:T(8,128)S(1)} %get-tuple-element.707), kind=kLoop, calls=%fused_computation.20.clone.1 | loop fusion | flops 4702208 | bytes 213504 | tf_op jit(solution)/shard_map/while/body/eval_jaxpr/tef,ef->tf/dot_general | solution.py:61
  37.1 0.7 dynamic_slice.82
  38.6 9.6 %fusion.156 = (f32[128,32]{0,1:T(8,128)S(1)}, f32[128,32]{0,1:T(8,128)S(1)}, f32[128,32]{0,1:T(8,128)S(1)}, f32[128,32]{0,1:T(8,128)S(1)}) fusion(f32[128,128]{0,1:T(8,128)S(1)} %get-tuple-element.706, f32[128]{0:T(128)S(1)} %multiply_add_fusion.11, f32[32,128]{1,0:T(8,128)S(1)} %add_divide_fusion.10, f32[128,128]{0,1:T(8,128)S(1)} %get-tuple-element.707), kind=kLoop, calls=%fused_computation.20.clone.1 | loop fusion | flops 4702208 | bytes 213504 | tf_op jit(solution)/shard_map/while/body/eval_jaxpr/tef,ef->tf/dot_general | solution.py:61
  48.3 0.7 dynamic_slice.82
  49.8 9.6 %fusion.156 = (f32[128,32]{0,1:T(8,128)S(1)}, f32[128,32]{0,1:T(8,128)S(1)}, f32[128,32]{0,1:T(8,128)S(1)}, f32[128,32]{0,1:T(8,128)S(1)}) fusion(f32[128,128]{0,1:T(8,128)S(1)} %get-tuple-element.706, f32[128]{0:T(128)S(1)} %multiply_add_fusion.11, f32[32,128]{1,0:T(8,128)S(1)} %add_divide_fusion.10, f32[128,128]{0,1:T(8,128)S(1)} %get-tuple-element.707), kind=kLoop, calls=%fused_computation.20.clone.1 | loop fusion | flops 4702208 | bytes 213504 | tf_op jit(solution)/shard_map/while/body/eval_jaxpr/tef,ef->tf/dot_general | solution.py:61
  59.5 33.5 %while.56 = (s32[]{:T(128)}, f32[32,256]{1,0:T(8,128)S(1)}, s32[3]{0:T(128)S(1)}, f32[384,128]{1,0:T(8,128)S(1)}, f32[384,128]{1,0:T(8,128)S(1)}, /*index=5*/s32...) while((s32[]{:T(128)}, f32[32,256]{1,0:T(8,128)S(1)}, ...), condition=%wide.region_3.4_spmd.clone, body=%wide.region_2.3_spmd.clone.sunk | while | flops 4756584 | bytes 690645 | solution.py:70
  59.5 0.7 dynamic_slice.84
  61.0 9.6 %fusion.157 = (f32[128,32]{0,1:T(8,128)S(1)}, f32[128,32]{0,1:T(8,128)S(1)}, f32[128,32]{0,1:T(8,128)S(1)}, f32[128,32]{0,1:T(8,128)S(1)}) fusion(f32[128,128]{0,1:T(8,128)S(1)} %get-tuple-element.719, f32[128]{0:T(128)S(1)} %multiply_add_fusion.12, f32[32,128]{1,0:T(8,128)S(1)} %add_divide_fusion.11, f32[128,128]{0,1:T(8,128)S(1)} %get-tuple-element.720), kind=kLoop, calls=%fused_computation.41.clone.1 | loop fusion | flops 4702208 | bytes 213504 | tf_op jit(solution)/shard_map/while/body/eval_jaxpr/tef,ef->tf/dot_general | solution.py:61
  70.7 0.7 dynamic_slice.84
  72.2 9.6 %fusion.157 = (f32[128,32]{0,1:T(8,128)S(1)}, f32[128,32]{0,1:T(8,128)S(1)}, f32[128,32]{0,1:T(8,128)S(1)}, f32[128,32]{0,1:T(8,128)S(1)}) fusion(f32[128,128]{0,1:T(8,128)S(1)} %get-tuple-element.719, f32[128]{0:T(128)S(1)} %multiply_add_fusion.12, f32[32,128]{1,0:T(8,128)S(1)} %add_divide_fusion.11, f32[128,128]{0,1:T(8,128)S(1)} %get-tuple-element.720), kind=kLoop, calls=%fused_computation.41.clone.1 | loop fusion | flops 4702208 | bytes 213504 | tf_op jit(solution)/shard_map/while/body/eval_jaxpr/tef,ef->tf/dot_general | solution.py:61
  81.9 0.7 dynamic_slice.84
  83.4 9.6 %fusion.157 = (f32[128,32]{0,1:T(8,128)S(1)}, f32[128,32]{0,1:T(8,128)S(1)}, f32[128,32]{0,1:T(8,128)S(1)}, f32[128,32]{0,1:T(8,128)S(1)}) fusion(f32[128,128]{0,1:T(8,128)S(1)} %get-tuple-element.719, f32[128]{0:T(128)S(1)} %multiply_add_fusion.12, f32[32,128]{1,0:T(8,128)S(1)} %add_divide_fusion.11, f32[128,128]{0,1:T(8,128)S(1)} %get-tuple-element.720), kind=kLoop, calls=%fused_computation.41.clone.1 | loop fusion | flops 4702208 | bytes 213504 | tf_op jit(solution)/shard_map/while/body/eval_jaxpr/tef,ef->tf/dot_general | solution.py:61
  93.0 3.6 %collective-permute-start.2 = (bf16[384,256]{1,0:T(8,128)(2,1)S(1)}, bf16[384,256]{1,0:T(8,128)(2,1)S(1)}, u32[]{:S(2)}, u32[]{:S(2)}) collective-permute-start(bf16[384,256]{1,0:T(8,128)(2,1)S(1)} %collective-permute-done), channel_id=1, source_target_pairs={{0,1},{1,2},{2,3},{3,4},{4,5},{5,6},{6,7},{7,8},{8,9},{9,10},{10,1... | collective-permute-start | bytes 589832 | tf_op jit(solution)/shard_map/ppermute | solution.py:25
  96.7 33.5 %while.57 = (s32[]{:T(128)}, f32[32,256]{1,0:T(8,128)S(1)}, s32[3]{0:T(128)S(1)}, f32[384,128]{1,0:T(8,128)S(1)}, f32[384,128]{1,0:T(8,128)S(1)}, /*index=5*/s32...) while((s32[]{:T(128)}, f32[32,256]{1,0:T(8,128)S(1)}, ...), condition=%wide.region_5.6_spmd.clone, body=%wide.region_4.5_spmd.clone.sunk | while | flops 4756583 | bytes 690625 | solution.py:70
  96.7 0.7 dynamic_slice.86
  98.3 9.6 %fusion.158 = (f32[128,32]{0,1:T(8,128)S(1)}, f32[128,32]{0,1:T(8,128)S(1)}, f32[128,32]{0,1:T(8,128)S(1)}, f32[128,32]{0,1:T(8,128)S(1)}) fusion(f32[128,128]{0,1:T(8,128)S(1)} %get-tuple-element.732, f32[128]{0:T(128)S(1)} %multiply_add_fusion.13, f32[32,128]{1,0:T(8,128)S(1)} %add_divide_fusion.12, f32[128,128]{0,1:T(8,128)S(1)} %get-tuple-element.733), kind=kLoop, calls=%fused_computation.62.clone.1 | loop fusion | flops 4702208 | bytes 213504 | tf_op jit(solution)/shard_map/while/body/eval_jaxpr/tef,ef->tf/dot_general | solution.py:61
  107.9 0.7 dynamic_slice.86
  109.4 9.6 %fusion.158 = (f32[128,32]{0,1:T(8,128)S(1)}, f32[128,32]{0,1:T(8,128)S(1)}, f32[128,32]{0,1:T(8,128)S(1)}, f32[128,32]{0,1:T(8,128)S(1)}) fusion(f32[128,128]{0,1:T(8,128)S(1)} %get-tuple-element.732, f32[128]{0:T(128)S(1)} %multiply_add_fusion.13, f32[32,128]{1,0:T(8,128)S(1)} %add_divide_fusion.12, f32[128,128]{0,1:T(8,128)S(1)} %get-tuple-element.733), kind=kLoop, calls=%fused_computation.62.clone.1 | loop fusion | flops 4702208 | bytes 213504 | tf_op jit(solution)/shard_map/while/body/eval_jaxpr/tef,ef->tf/dot_general | solution.py:61
  119.1 0.7 dynamic_slice.86
  120.6 9.6 %fusion.158 = (f32[128,32]{0,1:T(8,128)S(1)}, f32[128,32]{0,1:T(8,128)S(1)}, f32[128,32]{0,1:T(8,128)S(1)}, f32[128,32]{0,1:T(8,128)S(1)}) fusion(f32[128,128]{0,1:T(8,128)S(1)} %get-tuple-element.732, f32[128]{0:T(128)S(1)} %multiply_add_fusion.13, f32[32,128]{1,0:T(8,128)S(1)} %add_divide_fusion.12, f32[128,128]{0,1:T(8,128)S(1)} %get-tuple-element.733), kind=kLoop, calls=%fused_computation.62.clone.1 | loop fusion | flops 4702208 | bytes 213504 | tf_op jit(solution)/shard_map/while/body/eval_jaxpr/tef,ef->tf/dot_general | solution.py:61
  130.3 4.6 %collective-permute-start.3 = (bf16[384,256]{1,0:T(8,128)(2,1)S(1)}, bf16[384,256]{1,0:T(8,128)(2,1)S(1)}, u32[]{:S(2)}, u32[]{:S(2)}) collective-permute-start(bf16[384,256]{1,0:T(8,128)(2,1)S(1)} %collective-permute-done.1), channel_id=1, source_target_pairs={{1,0},{2,1},{3,2},{4,3},{5,4},{6,5},{7,6},{8,7},{9,8},{10,9},{11,1... | collective-permute-start | bytes 589832 | tf_op jit(solution)/shard_map/ppermute | solution.py:25
  135.0 33.4 %while.58 = (s32[]{:T(128)}, f32[32,256]{1,0:T(8,128)S(1)}, s32[3]{0:T(128)S(1)}, f32[384,128]{1,0:T(8,128)S(1)}, f32[384,128]{1,0:T(8,128)S(1)}, /*index=5*/s32...) while((s32[]{:T(128)}, f32[32,256]{1,0:T(8,128)S(1)}, ...), condition=%wide.region_7.8_spmd.clone, body=%wide.region_6.7_spmd.clone.sunk | while | flops 4756584 | bytes 690645 | solution.py:70
  136.5 9.5 %fusion.159 = (f32[128,32]{0,1:T(8,128)S(1)}, f32[128,32]{0,1:T(8,128)S(1)}, f32[128,32]{0,1:T(8,128)S(1)}, f32[128,32]{0,1:T(8,128)S(1)}) fusion(f32[128,128]{0,1:T(8,128)S(1)} %get-tuple-element.745, f32[128]{0:T(128)S(1)} %multiply_add_fusion.14, f32[32,128]{1,0:T(8,128)S(1)} %add_divide_fusion.13, f32[128,128]{0,1:T(8,128)S(1)} %get-tuple-element.746), kind=kLoop, calls=%fused_computation.83.clone.1 | loop fusion | flops 4702208 | bytes 213504 | tf_op jit(solution)/shard_map/while/body/eval_jaxpr/tef,ef->tf/dot_general | solution.py:61
  147.7 9.5 %fusion.159 = (f32[128,32]{0,1:T(8,128)S(1)}, f32[128,32]{0,1:T(8,128)S(1)}, f32[128,32]{0,1:T(8,128)S(1)}, f32[128,32]{0,1:T(8,128)S(1)}) fusion(f32[128,128]{0,1:T(8,128)S(1)} %get-tuple-element.745, f32[128]{0:T(128)S(1)} %multiply_add_fusion.14, f32[32,128]{1,0:T(8,128)S(1)} %add_divide_fusion.13, f32[128,128]{0,1:T(8,128)S(1)} %get-tuple-element.746), kind=kLoop, calls=%fused_computation.83.clone.1 | loop fusion | flops 4702208 | bytes 213504 | tf_op jit(solution)/shard_map/while/body/eval_jaxpr/tef,ef->tf/dot_general | solution.py:61
  158.8 9.5 %fusion.159 = (f32[128,32]{0,1:T(8,128)S(1)}, f32[128,32]{0,1:T(8,128)S(1)}, f32[128,32]{0,1:T(8,128)S(1)}, f32[128,32]{0,1:T(8,128)S(1)}) fusion(f32[128,128]{0,1:T(8,128)S(1)} %get-tuple-element.745, f32[128]{0:T(128)S(1)} %multiply_add_fusion.14, f32[32,128]{1,0:T(8,128)S(1)} %add_divide_fusion.13, f32[128,128]{0,1:T(8,128)S(1)} %get-tuple-element.746), kind=kLoop, calls=%fused_computation.83.clone.1 | loop fusion | flops 4702208 | bytes 213504 | tf_op jit(solution)/shard_map/while/body/eval_jaxpr/tef,ef->tf/dot_general | solution.py:61
  168.5 33.4 %while.59 = (s32[]{:T(128)}, f32[32,256]{1,0:T(8,128)S(1)}, s32[3]{0:T(128)S(1)}, f32[384,128]{1,0:T(8,128)S(1)}, f32[384,128]{1,0:T(8,128)S(1)}, /*index=5*/s32...) while((s32[]{:T(128)}, f32[32,256]{1,0:T(8,128)S(1)}, ...), condition=%wide.region_9.10_spmd.clone, body=%wide.region_8.9_spmd.clone.sunk | while | flops 4756584 | bytes 690645 | solution.py:70
  168.5 0.7 dynamic_slice.90
  170.0 9.5 %fusion.160 = (f32[128,32]{0,1:T(8,128)S(1)}, f32[128,32]{0,1:T(8,128)S(1)}, f32[128,32]{0,1:T(8,128)S(1)}, f32[128,32]{0,1:T(8,128)S(1)}) fusion(f32[128,128]{0,1:T(8,128)S(1)} %get-tuple-element.758, f32[128]{0:T(128)S(1)} %multiply_add_fusion.15, f32[32,128]{1,0:T(8,128)S(1)} %add_divide_fusion.14, f32[128,128]{0,1:T(8,128)S(1)} %get-tuple-element.759), kind=kLoop, calls=%fused_computation.104.clone.1 | loop fusion | flops 4702208 | bytes 213504 | tf_op jit(solution)/shard_map/while/body/eval_jaxpr/tef,ef->tf/dot_general | solution.py:61
  179.6 0.7 dynamic_slice.90
  181.1 9.5 %fusion.160 = (f32[128,32]{0,1:T(8,128)S(1)}, f32[128,32]{0,1:T(8,128)S(1)}, f32[128,32]{0,1:T(8,128)S(1)}, f32[128,32]{0,1:T(8,128)S(1)}) fusion(f32[128,128]{0,1:T(8,128)S(1)} %get-tuple-element.758, f32[128]{0:T(128)S(1)} %multiply_add_fusion.15, f32[32,128]{1,0:T(8,128)S(1)} %add_divide_fusion.14, f32[128,128]{0,1:T(8,128)S(1)} %get-tuple-element.759), kind=kLoop, calls=%fused_computation.104.clone.1 | loop fusion | flops 4702208 | bytes 213504 | tf_op jit(solution)/shard_map/while/body/eval_jaxpr/tef,ef->tf/dot_general | solution.py:61
  190.8 0.7 dynamic_slice.90
  192.3 9.5 %fusion.160 = (f32[128,32]{0,1:T(8,128)S(1)}, f32[128,32]{0,1:T(8,128)S(1)}, f32[128,32]{0,1:T(8,128)S(1)}, f32[128,32]{0,1:T(8,128)S(1)}) fusion(f32[128,128]{0,1:T(8,128)S(1)} %get-tuple-element.758, f32[128]{0:T(128)S(1)} %multiply_add_fusion.15, f32[32,128]{1,0:T(8,128)S(1)} %add_divide_fusion.14, f32[128,128]{0,1:T(8,128)S(1)} %get-tuple-element.759), kind=kLoop, calls=%fused_computation.104.clone.1 | loop fusion | flops 4702208 | bytes 213504 | tf_op jit(solution)/shard_map/while/body/eval_jaxpr/tef,ef->tf/dot_general | solution.py:61
  201.9 1.0 fusion.85
  203.0 13.9 %reduce-scatter.2.cloned.1.call-done = f32[32,256]{1,0:T(8,128)} async-done(((f32[32,512]{1,0:T(8,128)}), f32[32,256]{1,0:T(8,128)}) %reduce-scatter.2.cloned.1.call-update) | async-done | bytes 32784 | tf_op jit(solution)/shard_map/reduce_scatter | solution.py:140
  216.8 0.7 fusion.129
  217.6 3.1 %collective-permute-start.4 = (f32[16,128]{1,0:T(8,128)S(1)}, f32[16,128]{1,0:T(8,128)S(1)}, u32[]{:S(2)}, u32[]{:S(2)}) collective-permute-start(f32[16,128]{1,0:T(8,128)S(1)} %slice.124), channel_id=1, source_target_pairs={{1,0},{2,1},{3,2},{4,3},{5,4},{6,5},{7,6},{8,7},{9,8},{10,9},{11,1... | collective-permute-start | bytes 24584 | tf_op jit(solution)/shard_map/ppermute | solution.py:25
  220.7 1.9 collective-permute-done.4
  222.5 0.8 convolution_multiply_fusion
  (157 shorter events, 5.2 us)
Async XLA Ops:
  6.5 2.0 copy-start
  10.3 9.4 %all-to-all-start = ((bf16[192,2,256]{2,0,1:T(8,128)(2,1)}), bf16[192,2,256]{2,0,1:T(8,128)(2,1)S(1)}, u32[]{:S(2)}, u32[]{:S(2)}) async-start(bf16[192,2,256]{2,0,1:T(8,128)(2,1)} %bitcast.173), calls=%async_computation | async-start | bytes 393216 | tf_op jit(solution)/shard_map/all_to_all | solution.py:101
  14.5 202.4 %reduce-scatter.2.cloned.1.call-start = ((), (), s32[]{:S(2)}) async-start(), calls=%async_computation.2 | async-start | bytes 98304 | tf_op jit(solution)/shard_map/reduce_scatter | solution.py:140
  19.6 39.8 %collective-permute-start = (bf16[384,256]{1,0:T(8,128)(2,1)S(1)}, bf16[384,256]{1,0:T(8,128)(2,1)S(1)}, u32[]{:S(2)}, u32[]{:S(2)}) collective-permute-start(bf16[384,256]{1,0:T(8,128)(2,1)S(1)} %bitcast.231), channel_id=1, source_target_pairs={{0,1},{1,2},{2,3},{3,4},{4,5},{5,6},{6,7},{7,8},{8,9},{9,10},{10,1... | collective-permute-start | bytes 589832 | tf_op jit(solution)/shard_map/ppermute | solution.py:25
  23.9 72.8 %collective-permute-start.1 = (bf16[384,256]{1,0:T(8,128)(2,1)S(1)}, bf16[384,256]{1,0:T(8,128)(2,1)S(1)}, u32[]{:S(2)}, u32[]{:S(2)}) collective-permute-start(bf16[384,256]{1,0:T(8,128)(2,1)S(1)} %bitcast.232), channel_id=1, source_target_pairs={{1,0},{2,1},{3,2},{4,3},{5,4},{6,5},{7,6},{8,7},{9,8},{10,9},{11,1... | collective-permute-start | bytes 589832 | tf_op jit(solution)/shard_map/ppermute | solution.py:25
  93.0 41.9 %collective-permute-start.2 = (bf16[384,256]{1,0:T(8,128)(2,1)S(1)}, bf16[384,256]{1,0:T(8,128)(2,1)S(1)}, u32[]{:S(2)}, u32[]{:S(2)}) collective-permute-start(bf16[384,256]{1,0:T(8,128)(2,1)S(1)} %collective-permute-done), channel_id=1, source_target_pairs={{0,1},{1,2},{2,3},{3,4},{4,5},{5,6},{6,7},{7,8},{8,9},{9,10},{10,1... | collective-permute-start | bytes 589832 | tf_op jit(solution)/shard_map/ppermute | solution.py:25
  130.3 38.1 %collective-permute-start.3 = (bf16[384,256]{1,0:T(8,128)(2,1)S(1)}, bf16[384,256]{1,0:T(8,128)(2,1)S(1)}, u32[]{:S(2)}, u32[]{:S(2)}) collective-permute-start(bf16[384,256]{1,0:T(8,128)(2,1)S(1)} %collective-permute-done.1), channel_id=1, source_target_pairs={{1,0},{2,1},{3,2},{4,3},{5,4},{6,5},{7,6},{8,7},{9,8},{10,9},{11,1... | collective-permute-start | bytes 589832 | tf_op jit(solution)/shard_map/ppermute | solution.py:25
  201.9 18.8 %copy-start.1 = (s32[4]{0:T(128)S(1)}, s32[4]{0:T(128)}, u32[]{:S(2)}) copy-start(s32[4]{0:T(128)} %param.17) | copy-start | bytes 52
  217.6 5.0 %collective-permute-start.4 = (f32[16,128]{1,0:T(8,128)S(1)}, f32[16,128]{1,0:T(8,128)S(1)}, u32[]{:S(2)}, u32[]{:S(2)}) collective-permute-start(f32[16,128]{1,0:T(8,128)S(1)} %slice.124), channel_id=1, source_target_pairs={{1,0},{2,1},{3,2},{4,3},{5,4},{6,5},{7,6},{8,7},{9,8},{10,9},{11,1... | collective-permute-start | bytes 24584 | tf_op jit(solution)/shard_map/ppermute | solution.py:25
Sparse Core Ops, SparseCore 0:
  203.1 13.7 reduce-scatter.1
where the time goes:
time: 232 us; the launch traced here: 230 us
  other arithmetic  149 us (64%)
  starting transfers between devices  21.7 us (9%)
  waiting for transfers between devices  18.9 us (8%)
  between operations  15 us (6%)
  loops' own time  11.8 us (5%)
  local copies, waits for them, and re-layouts  11 us (5%)
  matrix products  2.67 us (1%)
    dot_general x15, other arithmetic, add_part(): jnp.einsum('tef,ef->tf', sin_kernel, rows_imag)  143 us
    ppermute x5, starting transfers between devices, from_behind(): lax.ppermute(value, axis, [(source, source + steps) for source in range(f...  17.5 us
    reduce_scatter x1, waiting for transfers between devices, per_device(): lax.psum_scatter(partial_field, 'section', scatter_dimension=1, tiled=True)  13.9 us
    another operation x5, loops' own time, kernel_sum(): lax.scan(add_part, initial, jnp.arange(echo_count // part_rows, dtype=jnp...  11.8 us
    dynamic_slice x15, local copies, waits for them, and re-layouts, kernel_sum(): lax.scan(add_part, initial, jnp.arange(echo_count // part_rows, dtype=jnp...  9.99 us
  transfers between devices with their start and end apart: 7, of which 3 were waited for; matrix products, arithmetic and copies ran while one was open for 54% of the time, Pallas kernels for 0%

commit v1 on v0

v1 whole, which is shorter than its diff:
```python
import functools
import math

import jax
import jax.numpy as jnp
import numpy as np
from jax import lax
from jax.experimental import pallas as pl
from jax.experimental.pallas import tpu as pltpu
from jax.sharding import PartitionSpec as P

SAMP = 256
ECH_DEV = 384
TB = 32
LOOK = 16
NBLK = 64
STEP = ECH_DEV // TB
HALF = ECH_DEV // 2
SUB = HALF // STEP
ROWS = 192
NFFT = 208
CHUNK = 16
WIN = 80
EXT = 48
VGRP = 4
FWD_AT = 1024
INV_AT = FWD_AT + VGRP * NFFT
RANGE_AT = INV_AT + 4 * ROWS
BF = jnp.bfloat16
F32 = jnp.float32


def split_bf16(x):
    hi = x.astype(np.float32).astype(jnp.bfloat16)
    lo = (x - hi.astype(np.float64)).astype(np.float32).astype(jnp.bfloat16)
    return np.stack([hi, lo])


@functools.lru_cache(maxsize=None)
def tables():
    s = np.arange(SAMP)
    psi = -math.pi * 0.37 * (s - SAMP // 2) ** 2 / SAMP
    turns = np.outer(s, s) % SAMP
    comp = np.exp(1j * psi)[:, None] * np.exp(-2j * math.pi * turns / SAMP) / math.sqrt(SAMP)
    comp = np.block([[comp.real, comp.imag], [-comp.imag, comp.real]])
    comp = split_bf16(comp)

    w = np.arange(NFFT)
    u = np.arange(SUB)
    fwd = np.exp(-2j * math.pi * (np.outer(w, u) % NFFT) / NFFT)
    cols = [[fwd.real, -fwd.imag], [fwd.imag, fwd.real]]
    lhs = np.zeros((VGRP, 2, NFFT, 2, VGRP, SUB))
    for v in range(VGRP):
        for o in range(2):
            for c in range(2):
                lhs[v, o, :, c, v, :] = cols[o][c]
    lhs = lhs.reshape(VGRP * 2 * NFFT, 2 * VGRP * SUB)
    hl = split_bf16(lhs)
    fwd_table = np.concatenate([hl[0], hl[1]], 1)

    f = np.arange(SAMP)
    kappa = 568.6 + (f - SAMP // 2) * 13.4 / SAMP
    resp = []
    for sec in range(2):
        j = sec * SUB - 127 + np.arange(NFFT)
        dist = (STEP * j[None, :] + np.arange(STEP)[:, None]) * (1200.0 / ECH_DEV)
        delay = dist * dist / (np.sqrt(1.3e6 * 1.3e6 + dist * dist) + 1.3e6)
        h = np.exp(-1j * delay[:, :, None] * kappa)
        h = np.roll(h, (sec * SUB - 127) % NFFT, axis=1)
        spec = np.fft.ifft(h, axis=1)
        shift = np.exp(-2j * math.pi * ((w * (SUB * sec + 64)) % NFFT) / NFFT)
        spec = spec * shift[None, :, None] / math.sqrt(4 * ECH_DEV)
        parts = np.stack([spec.real, spec.imag], 1)
        parts = parts.reshape(STEP, 2, NFFT // CHUNK, CHUNK, SAMP)
        resp.append(parts.transpose(2, 0, 1, 3, 4).reshape(NFFT // CHUNK, STEP * 2 * CHUNK, SAMP))
    resp = np.stack(resp).astype(np.float32)

    r = np.arange(ROWS)
    inv = np.exp(2j * math.pi * (np.outer(r, w) % NFFT) / NFFT)
    inv = np.block([[inv.real, -inv.imag], [inv.imag, inv.real]])
    inv_table = split_bf16(inv)

    base = np.exp(2j * math.pi * turns / SAMP) / math.sqrt(SAMP)
    full = np.block([[base.real, base.imag], [-base.imag, base.real]])
    halves = [
        np.concatenate([full[:, h * 128 : h * 128 + 128], full[:, 256 + h * 128 : 384 + h * 128]], 1)
        for h in range(2)
    ]
    range_table = np.stack(
        [split_bf16(np.concatenate([halves[1 - sec], halves[sec]], 1)) for sec in range(2)]
    )
    inv_table = np.concatenate([inv_table, np.zeros((2, 2 * ROWS, 512 - 2 * NFFT), inv_table.dtype)], 2)
    fwd_table = np.concatenate([fwd_table[: VGRP * NFFT], fwd_table[VGRP * NFFT :]], 1)
    packed = [comp, fwd_table, inv_table, range_table]
    return np.concatenate([t.reshape(-1, 512) for t in packed], 0), resp


def dot(a, b):
    return jnp.dot(a, b, preferred_element_type=F32)


def focus_kernel(
    first_ref, low_ref, raw_hbm, tab_hbm, resp_hbm,
    own, mate, up, down,
    raw, comp_t, fwd_t, resp, inv_t, comp, rhs, spec, img, sems,
):
    section = lax.axis_index("section")
    block = lax.axis_index("track")
    chunks = NFFT // CHUNK
    pairs = [(raw_hbm, raw), (tab_hbm.at[:FWD_AT], comp_t), (tab_hbm.at[FWD_AT:INV_AT], fwd_t)]
    pairs += [(resp_hbm.at[section, i], resp.at[i]) for i in range(chunks)]
    pairs += [(tab_hbm.at[INV_AT:RANGE_AT], inv_t)]
    copies = [pltpu.make_async_copy(src, dst, sems.at[i]) for i, (src, dst) in enumerate(pairs)]
    for copy in copies:
        copy.start()
    copies[0].wait()
    copies[1].wait()
    echoes = dot(raw[...], comp_t[:512]) + dot(raw[...], comp_t[512:])
    for n in range(4):
        comp[n] = echoes[:, n * 128 : n * 128 + 128]
    for v in range(STEP):
        rows = [comp[n, pl.ds(v, SUB, stride=STEP), :].astype(BF) for n in range(4)]
        q, i = divmod(v, VGRP)
        for c in range(2):
            part = jnp.concatenate(rows[2 * c : 2 * c + 2], 1)
            for d in range(2):
                at = ((d * 2 + c) * VGRP + i) * SUB
                rhs[q, at : at + SUB, :] = part
    copies[2].wait()
    for q in range(STEP // VGRP):
        for n in range(2):
            spec[q, n * VGRP * NFFT : (n + 1) * VGRP * NFFT] = dot(fwd_t[:, n * SAMP : (n + 1) * SAMP], rhs[q])
    for i in range(chunks):
        copies[3 + i].wait()
        sum_re = jnp.zeros((CHUNK, SAMP), F32)
        sum_im = jnp.zeros((CHUNK, SAMP), F32)
        for v in range(STEP):
            q, k = divmod(v, VGRP)
            at = k * 2 * NFFT + i * CHUNK
            y_re = spec[q, at : at + CHUNK, :]
            y_im = spec[q, at + NFFT : at + NFFT + CHUNK, :]
            h_re = resp[i, v * 2 * CHUNK : v * 2 * CHUNK + CHUNK, :]
            h_im = resp[i, v * 2 * CHUNK + CHUNK : (v + 1) * 2 * CHUNK, :]
            sum_re += y_re * h_re - y_im * h_im
            sum_im += y_re * h_im + y_im * h_re
        for n, total in enumerate((sum_re, sum_im)):
            hi = total.astype(BF)
            at = n * NFFT + i * CHUNK
            img[0, at : at + CHUNK, :] = hi
            img[1, at : at + CHUNK, :] = (total - hi.astype(F32)).astype(BF)
    copies[3 + chunks].wait()
    inv_hi = inv_t[: 2 * ROWS, : 2 * NFFT]
    inv_lo = inv_t[2 * ROWS :, : 2 * NFFT]
    image = dot(inv_hi, img[0]) + (dot(inv_lo, img[0]) + dot(inv_hi, img[1]))
    image = jnp.concatenate([image[:ROWS], image[ROWS:]], 1)
    own[...] = image[64 : 64 + WIN]
    narrow = image.astype(BF)
    up[...] = narrow[96:]
    down[:112, :] = narrow[:112]
    lane = lax.broadcasted_iota(jnp.int32, (16, 2 * SAMP), 1)
    first = (first_ref[0] - block * TB).astype(F32)
    flag = (low_ref[0] - block + 2).astype(F32)
    info = jnp.where(lane < SAMP, first, flag).astype(BF)
    down[112:, :] = info
    mate[:WIN, :] = jnp.where(block % 2 == 0, image[96 : 96 + WIN], image[32 : 32 + WIN]).astype(BF)
    mate[WIN:, :] = info


def join_kernel(low_ref, own, mate, up, down, across, swap_up, swap_down, tab_hbm, send, keep, nxt, table, sem):
    section = lax.axis_index("section")
    block = lax.axis_index("track")
    copy = pltpu.make_async_copy(tab_hbm.at[pl.ds(RANGE_AT + section * 1024, 1024)], table, sem)
    copy.start()
    even = block % 2 == 0
    near_mate = mate[:WIN, :].astype(F32)
    below = jnp.where(even, swap_up[:WIN, :].astype(F32), near_mate)
    above = jnp.where(even, near_mate, swap_down[32:112, :].astype(F32))
    far = jnp.where(even, swap_down[:EXT, :].astype(F32), across[...].astype(F32))
    info = jnp.where(even, mate[WIN:, :].astype(F32), swap_down[112:, :].astype(F32))[:8]
    nxt[...] = info[:, 128:384]
    next_low = info[0:1, SAMP : SAMP + 128] < 0.5
    next_low = jnp.concatenate([next_low] * 4, 1)
    low = low_ref[0] == block - 2
    here = own[...]
    two_up = down[:WIN, :].astype(F32)
    window = below[:64] + here[:64] + above[:64] + jnp.where(low, up[32:, :].astype(F32), two_up[:64])
    beyond = here[32:] + above[32:] + two_up[32:] + jnp.where(next_low, below[32:], far)
    image = jnp.concatenate([window, beyond], 0)
    hi = image.astype(BF)
    lo = (image - hi.astype(F32)).astype(BF)
    copy.wait()
    field = dot(hi, table[:512]) + (dot(lo, table[:512]) + dot(hi, table[512:]))
    send[...] = field[:, :256].astype(BF)
    keep[...] = field[:, 256:]


def look_kernel(first_ref, start_ref, keep, got, nxt, looks):
    block = lax.axis_index("track")
    field = keep[...] + got[...].astype(F32)
    power = field[:, :128] * field[:, :128] + field[:, 128:] * field[:, 128:]
    row = lax.broadcasted_iota(jnp.int32, (64 + EXT, 128), 0)
    next_first = nxt[0:1, 0:128].astype(jnp.int32)
    near = row - (first_ref[0] - block * TB)
    far = row - 64 - next_first + TB
    near = jnp.where((near >= 0) & (near < TB), near, -1)
    far = jnp.where((far >= TB) & (block < NBLK - 1), far, -1)
    place = jnp.where(row < 64, near, far)
    out = []
    for k in range(4):
        start = start_ref[k] - block * TB
        inside = (place >= start) & (place < start + LOOK)
        out.append(jnp.sum(jnp.where(inside, power, 0.0), 0, keepdims=True))
    looks[...] = jnp.concatenate(out, 0) * (1.0 / LOOK)


def shift(value, pairs):
    return lax.ppermute(value, ("section", "track"), pairs)


def both(pairs):
    return [(s * NBLK + a, s * NBLK + b) for s in range(2) for a, b in pairs]


def per_device(tab, resp, raw, first_target, aperture_first, look_start):
    vm = pl.BlockSpec(memory_space=pltpu.VMEM)
    sm = pl.BlockSpec(memory_space=pltpu.SMEM)
    hbm = pl.BlockSpec(memory_space=pltpu.HBM)
    own, mate, up, down = pl.pallas_call(
        focus_kernel,
        out_shape=[
            jax.ShapeDtypeStruct((WIN, 512), F32),
            jax.ShapeDtypeStruct((WIN + 16, 512), BF),
            jax.ShapeDtypeStruct((96, 512), BF),
            jax.ShapeDtypeStruct((128, 512), BF),
        ],
        in_specs=[sm, sm] + [hbm] * 3,
        out_specs=[vm] * 4,
        scratch_shapes=[
            pltpu.VMEM((HALF, 512), BF),
            pltpu.VMEM((FWD_AT, 512), BF),
            pltpu.VMEM((VGRP * NFFT, 512), BF),
            pltpu.VMEM((NFFT // CHUNK, STEP * 2 * CHUNK, SAMP), F32),
            pltpu.VMEM((4 * ROWS, 512), BF),
            pltpu.VMEM((4, HALF, 128), F32),
            pltpu.VMEM((STEP // VGRP, 256, SAMP), BF),
            pltpu.VMEM((STEP // VGRP, VGRP * 2 * NFFT, SAMP), F32),
            pltpu.VMEM((2, 2 * NFFT, SAMP), BF),
            pltpu.SemaphoreType.DMA((NFFT // CHUNK + 4,)),
        ],
        compiler_params=pltpu.CompilerParams(vmem_limit_bytes=52 * 1024 * 1024),
        name="focus",
    )(first_target, aperture_first, raw, tab, resp)
    from_below = shift(up, both([(t, t + 2) for t in range(NBLK - 2)]))
    from_above = shift(down, both([(t, t - 2) for t in range(2, NBLK)]))
    across = shift(down[:EXT], both([(t, t - 3) for t in range(4, NBLK, 2)]))
    swap = both([(t, t ^ 1) for t in range(NBLK)])
    mate = shift(mate, swap)
    swapped = shift(jnp.concatenate([from_below, from_above], 0), swap)
    send, keep, nxt = pl.pallas_call(
        join_kernel,
        out_shape=[
            jax.ShapeDtypeStruct((64 + EXT, 256), BF),
            jax.ShapeDtypeStruct((64 + EXT, 256), F32),
            jax.ShapeDtypeStruct((8, 256), F32),
        ],
        in_specs=[sm] + [vm] * 7 + [hbm],
        out_specs=[vm] * 3,
        scratch_shapes=[pltpu.VMEM((1024, 512), BF), pltpu.SemaphoreType.DMA],
        compiler_params=pltpu.CompilerParams(vmem_limit_bytes=32 * 1024 * 1024),
        name="join",
    )(aperture_first, own, mate, from_below, from_above, across, swapped[:96], swapped[96:], tab)
    got = shift(send, [(s * NBLK + t, (1 - s) * NBLK + t) for s in range(2) for t in range(NBLK)])
    return pl.pallas_call(
        look_kernel,
        out_shape=jax.ShapeDtypeStruct((4, 128), F32),
        in_specs=[sm, sm] + [vm] * 3,
        out_specs=vm,
        compiler_params=pltpu.CompilerParams(vmem_limit_bytes=4 * 1024 * 1024),
        name="look",
    )(first_target, look_start, keep, got, nxt)


def solution(mesh):
    consts = [jnp.asarray(t) for t in tables()]
    body = functools.partial(per_device, *consts)
    return jax.shard_map(
        body,
        mesh=mesh,
        in_specs=(P(("track", "section"), None), P("track"), P("track"), P("track")),
        out_specs=P("track", "section"),
        check_vma=False,
    )
```

time: 232 us -> 36.8 us (0.16)
  other arithmetic: 149 us -> 0.02 us
  between operations: 15 us -> 1.7 us
  loops' own time: 11.8 us -> 0 us
  local copies, waits for them, and re-layouts: 11 us -> 0.95 us
  starting transfers between devices: 21.7 us -> 15.1 us
  waiting for transfers between devices: 18.9 us -> 12.4 us
  Pallas kernels: 0 us -> 6.44 us
  matrix products: 2.67 us -> 0 us
    dot_general x15 -> x0, other arithmetic: 143 us -> none  [add_part(): jnp.einsum('tef,ef->tf', sin_kernel, rows_imag)]
    reduce_scatter x1 -> x0, waiting for transfers between devices: 13.9 us -> none  [per_device(): lax.psum_scatter(partial_field, 'section', scatter_dimension=1, tiled=True)]
    another operation x5 -> x0, loops' own time: 11.8 us -> none  [kernel_sum(): lax.scan(add_part, initial, jnp.arange(echo_count // part_rows, dtype=jnp...]
    ppermute x5 -> x6, waiting for transfers between devices: 1.88 us -> 12.4 us  [shift(): return lax.ppermute(value, ('section', 'track'), pairs)]
    dynamic_slice x15 -> x0, local copies, waits for them, and re-layouts: 9.99 us -> none  [kernel_sum(): lax.scan(add_part, initial, jnp.arange(echo_count // part_rows, dtype=jnp...]
    pallas_call x0 -> x3, Pallas kernels: none -> 6.44 us  [the longest x1 4.63 us: per_device(): pl.pallas_call(focus_kernel, out_shape=[jax.ShapeDtypeStruct((WIN, 512),...]
    all_to_all x1 -> x0, starting transfers between devices: 4.18 us -> none  [per_device(): lax.all_to_all(compressed, 'section', split_axis=1, concat_axis=0, tiled=...]
    all_to_all x1 -> x0, waiting for transfers between devices: 3.16 us -> none  [per_device(): lax.all_to_all(compressed, 'section', split_axis=1, concat_axis=0, tiled=...]
  transfers between devices with their start and end apart: 7 -> 6, of which waited for: 3 -> 3; matrix products, arithmetic and copies ran while one was open for 54% -> 0% of each run, Pallas kernels for 0% -> 0%
where the time goes in v1:
time: 36.8 us; the launch traced here: 36.7 us
  starting transfers between devices  15.1 us (41%)
  waiting for transfers between devices  12.4 us (34%)
  Pallas kernels  6.44 us (18%)
  between operations  1.7 us (5%)
  local copies, waits for them, and re-layouts  0.95 us (3%)
    ppermute x6, starting transfers between devices, shift(): return lax.ppermute(value, ('section', 'track'), pairs)  15.1 us
    ppermute x6, waiting for transfers between devices, shift(): return lax.ppermute(value, ('section', 'track'), pairs)  12.4 us
    pallas_call x1, Pallas kernels, per_device(): pl.pallas_call(focus_kernel, out_shape=[jax.ShapeDtypeStruct((WIN, 512),...  4.63 us
    pallas_call x1, Pallas kernels, per_device(): pl.pallas_call(look_kernel, out_shape=jax.ShapeDtypeStruct((4, 128), F32)...  1.2 us
    unnamed x8, local copies, waits for them, and re-layouts  0.93 us
  transfers between devices with their start and end apart: 6, of which 3 were waited for; matrix products, arithmetic and copies ran while one was open for 0% of the time, Pallas kernels for 0%

profile of v1, /device:TPU:7, one launch (start us, length us, event | category | flops | bytes accessed | tf_op | source)
XLA Modules:
  0.0 36.7 jit_solution(1578582179613023448)
XLA Ops:
  0.0 0.0 slice-start
  1.6 0.0 copy-start
  1.6 0.9 %copy-done = bf16[192,512]{1,0:T(8,128)(2,1)S(1)} copy-done((bf16[192,512]{1,0:T(8,128)(2,1)S(1)}, bf16[192,512]{1,0:T(8,128)(2,1)}, u32[]{:S(2)}) %copy-start) | copy-done | bytes 196632
  2.5 0.0 slice-start.1
  2.5 0.0 copy-start.1
  2.5 4.6 %focus.1 = (f32[80,512]{1,0:T(8,128)S(1)}, bf16[96,512]{1,0:T(8,128)(2,1)S(1)}, bf16[96,512]{1,0:T(8,128)(2,1)S(1)}, bf16[128,512]{1,0:T(8,128)(2,1)S(1)}) custom-call(s32[1]{0:T(128)S(6)} %copy.7.first_ref, s32[1]{0:T(128)S(6)} %copy.8.low_ref, bf16[192,512]{1,0:T(8,128)(2,1)S(1)} %copy-done, bf16[4672,512]{1,0:T(8,128)(2,1)} %constant.4.clone.tab_hbm, ...), custom_call_target="tpu_custom_call" | custom-call | tf_op jit(solution)/shard_map/focus/pallas_call | solution.py:228
  7.2 6.9 %collective-permute-start.2 = (bf16[128,512]{1,0:T(8,128)(2,1)S(1)}, bf16[128,512]{1,0:T(8,128)(2,1)S(1)}, u32[]{:S(2)}, u32[]{:S(2)}) collective-permute-start(bf16[128,512]{1,0:T(8,128)(2,1)S(1)} %get-tuple-element.15), channel_id=1, source_target_pairs={{2,0},{3,1},{4,2},{5,3},{6,4},{7,5},{8,6},{9,7},{10,8},{11,9},{12,... | collective-permute-start | bytes 393224 | tf_op jit(solution)/shard_map/ppermute | solution.py:217
  14.1 1.9 %collective-permute-start.1 = (bf16[96,512]{1,0:T(8,128)(2,1)S(1)}, bf16[96,512]{1,0:T(8,128)(2,1)S(1)}, u32[]{:S(2)}, u32[]{:S(2)}) collective-permute-start(bf16[96,512]{1,0:T(8,128)(2,1)S(1)} %get-tuple-element.14), channel_id=1, source_target_pairs={{0,2},{1,3},{2,4},{3,5},{4,6},{5,7},{6,8},{7,9},{8,10},{9,11},{10,... | collective-permute-start | bytes 294920 | tf_op jit(solution)/shard_map/ppermute | solution.py:217
  16.1 6.4 %collective-permute-done.1.up = bf16[96,512]{1,0:T(8,128)(2,1)S(1)} collective-permute-done((bf16[96,512]{1,0:T(8,128)(2,1)S(1)}, bf16[96,512]{1,0:T(8,128)(2,1)S(1)}, u32[]{:S(2)}, u32[]{:S(2)}) %collective-permute-start.1) | collective-permute-done | bytes 98336 | tf_op jit(solution)/shard_map/ppermute | solution.py:217
  22.5 0.0 collective-permute-done.2.down
  22.5 2.2 %collective-permute-start.4 = (bf16[224,512]{1,0:T(8,128)(2,1)S(1)}, bf16[224,512]{1,0:T(8,128)(2,1)S(1)}, u32[]{:S(2)}, u32[]{:S(2)}) collective-permute-start(bf16[224,512]{1,0:T(8,128)(2,1)S(1)} %pad_maximum_fusion), channel_id=1, source_target_pairs={{0,1},{1,0},{2,3},{3,2},{4,5},{5,4},{6,7},{7,6},{8,9},{9,8},{10,11... | collective-permute-start | bytes 688136 | tf_op jit(solution)/shard_map/ppermute | solution.py:217
  24.7 0.1 collective-permute-start
  24.8 1.3 %collective-permute-start.3 = (bf16[48,512]{1,0:T(8,128)(2,1)S(1)}, bf16[48,512]{1,0:T(8,128)(2,1)S(1)}, u32[]{:S(2)}, u32[]{:S(2)}) collective-permute-start(bf16[48,512]{1,0:T(8,128)(2,1)S(1)} %slice.9), channel_id=1, source_target_pairs={{4,1},{6,3},{8,5},{10,7},{12,9},{14,11},{16,13},{18,15},{20,17},{2... | collective-permute-start | bytes 147464 | tf_op jit(solution)/shard_map/ppermute | solution.py:217
  26.1 0.0 collective-permute-done.4
  26.1 4.1 %collective-permute-done.3.across = bf16[48,512]{1,0:T(8,128)(2,1)S(1)} collective-permute-done((bf16[48,512]{1,0:T(8,128)(2,1)S(1)}, bf16[48,512]{1,0:T(8,128)(2,1)S(1)}, u32[]{:S(2)}, u32[]{:S(2)}) %collective-permute-start.3) | collective-permute-done | bytes 49184 | tf_op jit(solution)/shard_map/ppermute | solution.py:217
  30.2 0.0 collective-permute-done.mate
  30.2 0.0 slice-done
  30.2 0.0 slice-done.1
  30.2 0.6 %join.1 = (bf16[112,256]{1,0:T(8,128)(2,1)S(1)}, f32[112,256]{1,0:T(8,128)S(1)}, f32[8,256]{1,0:T(8,128)S(1)}) custom-call(s32[1]{0:T(128)S(6)} %copy.8.low_ref, f32[80,512]{1,0:T(8,128)S(1)} %get-tuple-element.12.own, bf16[96,512]{1,0:T(8,128)(2,1)S(1)} %collective-permute-done.mate, bf16[96,512]{1,0:T(8,128)(2,1)S(1)} %collective-permute-done.1.up, ...), custom_call_target="tpu_custom_call" | custom-call | tf_op jit(solution)/shard_map/join/pallas_call | solution.py:259
  30.8 2.7 %collective-permute-start.5 = (bf16[112,256]{1,0:T(8,128)(2,1)S(1)}, bf16[112,256]{1,0:T(8,128)(2,1)S(1)}, u32[]{:S(2)}, u32[]{:S(2)}) collective-permute-start(bf16[112,256]{1,0:T(8,128)(2,1)S(1)} %get-tuple-element.17), channel_id=1, source_target_pairs={{0,64},{1,65},{2,66},{3,67},{4,68},{5,69},{6,70},{7,71},{8,72},{9,... | collective-permute-start | bytes 172040 | tf_op jit(solution)/shard_map/ppermute | solution.py:217
  33.6 1.9 %collective-permute-done.5.got = bf16[112,256]{1,0:T(8,128)(2,1)S(1)} collective-permute-done((bf16[112,256]{1,0:T(8,128)(2,1)S(1)}, bf16[112,256]{1,0:T(8,128)(2,1)S(1)}, u32[]{:S(2)}, u32[]{:S(2)}) %collective-permute-start.5) | collective-permute-done | bytes 57376 | tf_op jit(solution)/shard_map/ppermute | solution.py:217
  35.5 0.0 copy-done.1
  35.5 1.2 %look.1 = f32[4,128]{1,0:T(4,128)} custom-call(s32[1]{0:T(128)S(6)} %copy.7.first_ref, s32[4]{0:T(128)S(1)} %copy-done.1, f32[112,256]{1,0:T(8,128)S(1)} %get-tuple-element.16.keep, bf16[112,256]{1,0:T(8,128)(2,1)S(1)} %collective-permute-done.5.got, f32[8,256]{1,0:T(8,128)S(1)} %get-tuple-element.18.nxt), custom_call_target="tpu_custom_call" | custom-call | tf_op jit(solution)/shard_map/look/pallas_call | solution.py:273
  (5 shorter events, 0.0 us)
Async XLA Ops:
  0.0 30.2 %slice-start = ((s8[4784128]{0:T(1024)(128)(4,1)}), s8[4194304]{0:T(1024)(128)(4,1)S(1)}, s32[]{:S(2)}) async-start(s8[4784128]{0:T(1024)(128)(4,1)} %bitcast), calls=%async_computation | async-start | bytes 8388608
  1.6 0.9 %copy-start = (bf16[192,512]{1,0:T(8,128)(2,1)S(1)}, bf16[192,512]{1,0:T(8,128)(2,1)}, u32[]{:S(2)}) copy-start(bf16[192,512]{1,0:T(8,128)(2,1)} %raw_hbm.1) | copy-start | bytes 589828
  2.5 27.7 %slice-start.1 = ((s8[4784128]{0:T(1024)(128)(4,1)}), s8[589824]{0:T(1024)(128)(4,1)S(1)}, s32[]{:S(2)}) async-start(s8[4784128]{0:T(1024)(128)(4,1)} %bitcast), calls=%async_computation.1 | async-start | bytes 1179648
  2.5 32.9 %copy-start.1 = (s32[4]{0:T(128)S(1)}, s32[4]{0:T(128)}, u32[]{:S(2)}) copy-start(s32[4]{0:T(128)} %start_ref.1) | copy-start | bytes 52
  7.2 15.3 %collective-permute-start.2 = (bf16[128,512]{1,0:T(8,128)(2,1)S(1)}, bf16[128,512]{1,0:T(8,128)(2,1)S(1)}, u32[]{:S(2)}, u32[]{:S(2)}) collective-permute-start(bf16[128,512]{1,0:T(8,128)(2,1)S(1)} %get-tuple-element.15), channel_id=1, source_target_pairs={{2,0},{3,1},{4,2},{5,3},{6,4},{7,5},{8,6},{9,7},{10,8},{11,9},{12,... | collective-permute-start | bytes 393224 | tf_op jit(solution)/shard_map/ppermute | solution.py:217
  14.1 8.4 %collective-permute-start.1 = (bf16[96,512]{1,0:T(8,128)(2,1)S(1)}, bf16[96,512]{1,0:T(8,128)(2,1)S(1)}, u32[]{:S(2)}, u32[]{:S(2)}) collective-permute-start(bf16[96,512]{1,0:T(8,128)(2,1)S(1)} %get-tuple-element.14), channel_id=1, source_target_pairs={{0,2},{1,3},{2,4},{3,5},{4,6},{5,7},{6,8},{7,9},{8,10},{9,11},{10,... | collective-permute-start | bytes 294920 | tf_op jit(solution)/shard_map/ppermute | solution.py:217
  22.5 3.6 %collective-permute-start.4 = (bf16[224,512]{1,0:T(8,128)(2,1)S(1)}, bf16[224,512]{1,0:T(8,128)(2,1)S(1)}, u32[]{:S(2)}, u32[]{:S(2)}) collective-permute-start(bf16[224,512]{1,0:T(8,128)(2,1)S(1)} %pad_maximum_fusion), channel_id=1, source_target_pairs={{0,1},{1,0},{2,3},{3,2},{4,5},{5,4},{6,7},{7,6},{8,9},{9,8},{10,11... | collective-permute-start | bytes 688136 | tf_op jit(solution)/shard_map/ppermute | solution.py:217
  24.7 5.5 %collective-permute-start = (bf16[96,512]{1,0:T(8,128)(2,1)S(1)}, bf16[96,512]{1,0:T(8,128)(2,1)S(1)}, u32[]{:S(2)}, u32[]{:S(2)}) collective-permute-start(bf16[96,512]{1,0:T(8,128)(2,1)S(1)} %get-tuple-element.13), channel_id=1, source_target_pairs={{0,1},{1,0},{2,3},{3,2},{4,5},{5,4},{6,7},{7,6},{8,9},{9,8},{10,11... | collective-permute-start | bytes 294920 | tf_op jit(solution)/shard_map/ppermute | solution.py:217
  24.8 5.4 %collective-permute-start.3 = (bf16[48,512]{1,0:T(8,128)(2,1)S(1)}, bf16[48,512]{1,0:T(8,128)(2,1)S(1)}, u32[]{:S(2)}, u32[]{:S(2)}) collective-permute-start(bf16[48,512]{1,0:T(8,128)(2,1)S(1)} %slice.9), channel_id=1, source_target_pairs={{4,1},{6,3},{8,5},{10,7},{12,9},{14,11},{16,13},{18,15},{20,17},{2... | collective-permute-start | bytes 147464 | tf_op jit(solution)/shard_map/ppermute | solution.py:217
  30.8 4.6 %collective-permute-start.5 = (bf16[112,256]{1,0:T(8,128)(2,1)S(1)}, bf16[112,256]{1,0:T(8,128)(2,1)S(1)}, u32[]{:S(2)}, u32[]{:S(2)}) collective-permute-start(bf16[112,256]{1,0:T(8,128)(2,1)S(1)} %get-tuple-element.17), channel_id=1, source_target_pairs={{0,64},{1,65},{2,66},{3,67},{4,68},{5,69},{6,70},{7,71},{8,72},{9,... | collective-permute-start | bytes 172040 | tf_op jit(solution)/shard_map/ppermute | solution.py:217

commit v2 on v1

v2 whole, which is shorter than its diff:
```python
import functools
import math

import jax
import jax.numpy as jnp
import numpy as np
from jax import lax
from jax.experimental import pallas as pl
from jax.experimental.pallas import tpu as pltpu
from jax.sharding import PartitionSpec as P

SAMP = 256
ECH_DEV = 384
TB = 32
LOOK = 16
NBLK = 64
STEP = ECH_DEV // TB
HALF = ECH_DEV // 2
SUB = HALF // STEP
ROWS = 192
NFFT = 208
CHUNK = 16
WIN = 80
EXT = 48
VGRP = 4
FWD_AT = 512
INV_AT = FWD_AT + VGRP * NFFT
RANGE_AT = INV_AT + 4 * ROWS
TAB_END = RANGE_AT + 512
FOCUS_VMEM = 54912 * 1024
SMALL_VMEM = 8 * 1024 * 1024
BF = jnp.bfloat16
F32 = jnp.float32


def split_bf16(x):
    hi = x.astype(np.float32).astype(jnp.bfloat16)
    lo = (x - hi.astype(np.float64)).astype(np.float32).astype(jnp.bfloat16)
    return np.stack([hi, lo])


@functools.lru_cache(maxsize=None)
def tables():
    s = np.arange(SAMP)
    psi = -math.pi * 0.37 * (s - SAMP // 2) ** 2 / SAMP
    turns = np.outer(s, s) % SAMP
    comp = np.exp(1j * psi)[:, None] * np.exp(-2j * math.pi * turns / SAMP) / math.sqrt(SAMP)
    comp = split_bf16(np.concatenate([comp.real, comp.imag], 1))

    w = np.arange(NFFT)
    u = np.arange(SUB)
    fwd = np.exp(-2j * math.pi * (np.outer(w, u) % NFFT) / NFFT)
    cols = [[fwd.real, -fwd.imag], [fwd.imag, fwd.real]]
    lhs = np.zeros((VGRP, 2, NFFT, 2, VGRP, SUB))
    for v in range(VGRP):
        for o in range(2):
            for c in range(2):
                lhs[v, o, :, c, v, :] = cols[o][c]
    lhs = lhs.reshape(VGRP * 2 * NFFT, 2 * VGRP * SUB)
    hl = split_bf16(lhs)
    fwd_table = np.concatenate([hl[0], hl[1]], 1)

    f = np.arange(SAMP)
    kappa = 568.6 + (f - SAMP // 2) * 13.4 / SAMP
    resp = []
    for sec in range(2):
        j = sec * SUB - 127 + np.arange(NFFT)
        dist = (STEP * j[None, :] + np.arange(STEP)[:, None]) * (1200.0 / ECH_DEV)
        delay = dist * dist / (np.sqrt(1.3e6 * 1.3e6 + dist * dist) + 1.3e6)
        h = np.exp(-1j * delay[:, :, None] * kappa)
        h = np.roll(h, (sec * SUB - 127) % NFFT, axis=1)
        spec = np.fft.ifft(h, axis=1)
        shift = np.exp(-2j * math.pi * ((w * (SUB * sec + 64)) % NFFT) / NFFT)
        spec = spec * shift[None, :, None] / math.sqrt(4 * ECH_DEV)
        parts = np.stack([spec.real, spec.imag], 1)
        parts = parts.reshape(STEP, 2, NFFT // CHUNK, CHUNK, SAMP)
        resp.append(parts.transpose(2, 0, 1, 3, 4).reshape(NFFT // CHUNK, STEP * 2 * CHUNK, SAMP))
    resp = np.stack(resp).astype(np.float32)

    r = np.arange(ROWS)
    inv = np.exp(2j * math.pi * (np.outer(r, w) % NFFT) / NFFT)
    inv = np.block([[inv.real, -inv.imag], [inv.imag, inv.real]])
    inv_table = split_bf16(inv)

    base = np.exp(2j * math.pi * turns / SAMP) / math.sqrt(SAMP)
    range_table = split_bf16(np.concatenate([base.real, base.imag], 1))
    inv_table = np.concatenate([inv_table, np.zeros((2, 2 * ROWS, 512 - 2 * NFFT), inv_table.dtype)], 2)
    fwd_table = np.concatenate([fwd_table[: VGRP * NFFT], fwd_table[VGRP * NFFT :]], 1)
    packed = [comp, fwd_table, inv_table, range_table]
    return np.concatenate([t.reshape(-1, 512) for t in packed], 0), resp


def dot(a, b):
    return jnp.dot(a, b, preferred_element_type=F32)


def complex_dot(parts, table):
    rows = table.shape[0] // 2
    re, im = parts
    sums = []
    for part in (re, im):
        total = dot(part[0], table[:rows]) + dot(part[0], table[rows:])
        if len(part) > 1:
            total = total + dot(part[1], table[:rows])
        sums.append(total)
    width = table.shape[1] // 2
    return sums[0][:, :width] - sums[1][:, width:], sums[0][:, width:] + sums[1][:, :width]


def hi_lo(x):
    hi = x.astype(BF)
    return hi, (x - hi.astype(F32)).astype(BF)


def focus_kernel(
    raw_hbm, tab_hbm, resp_hbm,
    send, keep,
    raw, comp_t, fwd_t, resp, inv_t, range_t, comp, rhs, spec, img, sems,
):
    section = lax.axis_index("section")
    chunks = NFFT // CHUNK
    pairs = [(raw_hbm, raw), (tab_hbm.at[:FWD_AT], comp_t), (tab_hbm.at[FWD_AT:INV_AT], fwd_t)]
    pairs += [(resp_hbm.at[section, i], resp.at[i]) for i in range(chunks)]
    pairs += [(tab_hbm.at[INV_AT:RANGE_AT], inv_t), (tab_hbm.at[RANGE_AT:TAB_END], range_t)]
    copies = [pltpu.make_async_copy(src, dst, sems.at[i]) for i, (src, dst) in enumerate(pairs)]
    for copy in copies:
        copy.start()
    copies[0].wait()
    copies[1].wait()
    echo_re, echo_im = complex_dot([(raw[:, :SAMP],), (raw[:, SAMP:],)], comp_t[...])
    for n in range(2):
        comp[n] = echo_re[:, n * 128 : n * 128 + 128]
        comp[2 + n] = echo_im[:, n * 128 : n * 128 + 128]
    for v in range(STEP):
        rows = [comp[n, pl.ds(v, SUB, stride=STEP), :].astype(BF) for n in range(4)]
        q, i = divmod(v, VGRP)
        for c in range(2):
            part = jnp.concatenate(rows[2 * c : 2 * c + 2], 1)
            for d in range(2):
                at = ((d * 2 + c) * VGRP + i) * SUB
                rhs[q, at : at + SUB, :] = part
    copies[2].wait()
    for q in range(STEP // VGRP):
        for n in range(2):
            spec[q, n * VGRP * NFFT : (n + 1) * VGRP * NFFT] = dot(fwd_t[:, n * SAMP : (n + 1) * SAMP], rhs[q])
    for i in range(chunks):
        copies[3 + i].wait()
        sum_re = jnp.zeros((CHUNK, SAMP), F32)
        sum_im = jnp.zeros((CHUNK, SAMP), F32)
        for v in range(STEP):
            q, k = divmod(v, VGRP)
            at = k * 2 * NFFT + i * CHUNK
            y_re = spec[q, at : at + CHUNK, :]
            y_im = spec[q, at + NFFT : at + NFFT + CHUNK, :]
            h_re = resp[i, v * 2 * CHUNK : v * 2 * CHUNK + CHUNK, :]
            h_im = resp[i, v * 2 * CHUNK + CHUNK : (v + 1) * 2 * CHUNK, :]
            sum_re += y_re * h_re - y_im * h_im
            sum_im += y_re * h_im + y_im * h_re
        for n, total in enumerate((sum_re, sum_im)):
            hi = total.astype(BF)
            at = n * NFFT + i * CHUNK
            img[0, at : at + CHUNK, :] = hi
            img[1, at : at + CHUNK, :] = (total - hi.astype(F32)).astype(BF)
    copies[3 + chunks].wait()
    inv_hi = inv_t[: 2 * ROWS, : 2 * NFFT]
    inv_lo = inv_t[2 * ROWS :, : 2 * NFFT]
    image = dot(inv_hi, img[0]) + (dot(inv_lo, img[0]) + dot(inv_hi, img[1]))
    copies[4 + chunks].wait()
    field_re, field_im = complex_dot([hi_lo(image[:ROWS]), hi_lo(image[ROWS:])], range_t[...])
    low = jnp.concatenate([field_re[:, :128], field_im[:, :128]], 1)
    high = jnp.concatenate([field_re[:, 128:], field_im[:, 128:]], 1)

    @pl.when(section == 0)
    def low_half():
        send[...] = high.astype(BF)
        keep[...] = low

    @pl.when(section == 1)
    def high_half():
        send[...] = low.astype(BF)
        keep[...] = high


def mix_kernel(first_ref, low_ref, keep, got, own, mine, onward):
    block = lax.axis_index("track")
    lane = lax.broadcasted_iota(jnp.int32, (16, SAMP), 1)
    info = jnp.where(lane < 128, first_ref[0] - block * TB, low_ref[0] - block + 2)
    field = keep[...] + got[...].astype(F32)
    own[...] = field[64 : 64 + WIN]
    mine[112:128, :] = info.astype(F32).astype(BF)

    @pl.when(block % 2 == 0)
    def even():
        onward[...] = field[112:].astype(BF)
        mine[:112, :] = field[:112].astype(BF)
        mine[128:, :] = field[96:176].astype(BF)

    @pl.when(block % 2 == 1)
    def odd():
        onward[...] = field[:80].astype(BF)
        mine[:112, :] = field[80:].astype(BF)
        mine[128:, :] = field[32:112].astype(BF)


def look_kernel(starts, own, mine, mate, moved, swapped, looks):
    block = lax.axis_index("track")
    even = block % 2 == 0
    near = mate[128:, :].astype(F32)
    below = jnp.where(even, moved[96:176, :].astype(F32), near)
    above = jnp.where(even, near, moved[112:192, :].astype(F32))
    two_down = jnp.where(even, moved[16:80, :].astype(F32), swapped[128:192, :].astype(F32))
    two_up = jnp.where(even, swapped[80:160, :].astype(F32), moved[:80, :].astype(F32))
    far = jnp.where(even, swapped[:EXT, :].astype(F32), swapped[192:, :].astype(F32))
    next_info = jnp.where(even, mate[112:128, :].astype(F32), moved[192:, :].astype(F32))
    own_info = mine[112:128, :].astype(F32)
    first, next_first = own_info[0:1, :128], next_info[0:1, :128]
    low, next_low = own_info[0:1, 128:] < 0.5, next_info[0:1, 128:] < 0.5
    low = jnp.concatenate([low, low], 1)
    next_low = jnp.concatenate([next_low, next_low], 1)
    here = own[...]
    window = below[:64] + here[:64] + above[:64] + jnp.where(low, two_down, two_up[:64])
    beyond = here[32:] + above[32:] + two_up[32:] + jnp.where(next_low, below[32:], far)
    field = jnp.concatenate([window, beyond], 0)
    power = field[:, :128] * field[:, :128] + field[:, 128:] * field[:, 128:]
    row = lax.broadcasted_iota(jnp.int32, (64 + EXT, 128), 0)
    inner = row - first.astype(jnp.int32)
    outer = row - 64 - next_first.astype(jnp.int32) + TB
    inner = jnp.where((inner >= 0) & (inner < TB), inner, -1)
    outer = jnp.where((outer >= TB) & (block < NBLK - 1), outer, -1)
    place = jnp.where(row < 64, inner, outer)
    out = []
    for k in range(4):
        start = starts[:, k : k + 1] - block * TB
        inside = (place >= start) & (place < start + LOOK)
        out.append(jnp.sum(jnp.where(inside, power, 0.0), 0, keepdims=True))
    looks[...] = jnp.concatenate(out, 0) * (1.0 / LOOK)


def shift(value, pairs):
    return lax.ppermute(value, ("section", "track"), pairs)


def both(pairs):
    return [(s * NBLK + a, s * NBLK + b) for s in range(2) for a, b in pairs]


def per_device(tab, resp, raw, first_target, aperture_first, look_start):
    vm = pl.BlockSpec(memory_space=pltpu.VMEM)
    sm = pl.BlockSpec(memory_space=pltpu.SMEM)
    hbm = pl.BlockSpec(memory_space=pltpu.HBM)
    send, keep = pl.pallas_call(
        focus_kernel,
        out_shape=[
            jax.ShapeDtypeStruct((ROWS, SAMP), BF),
            jax.ShapeDtypeStruct((ROWS, SAMP), F32),
        ],
        in_specs=[hbm] * 3,
        out_specs=[vm] * 2,
        scratch_shapes=[
            pltpu.VMEM((HALF, 512), BF),
            pltpu.VMEM((FWD_AT, 512), BF),
            pltpu.VMEM((VGRP * NFFT, 512), BF),
            pltpu.VMEM((NFFT // CHUNK, STEP * 2 * CHUNK, SAMP), F32),
            pltpu.VMEM((4 * ROWS, 512), BF),
            pltpu.VMEM((512, 512), BF),
            pltpu.VMEM((4, HALF, 128), F32),
            pltpu.VMEM((STEP // VGRP, 256, SAMP), BF),
            pltpu.VMEM((STEP // VGRP, VGRP * 2 * NFFT, SAMP), F32),
            pltpu.VMEM((2, 2 * NFFT, SAMP), BF),
            pltpu.SemaphoreType.DMA((NFFT // CHUNK + 5,)),
        ],
        compiler_params=pltpu.CompilerParams(vmem_limit_bytes=FOCUS_VMEM),
        name="focus",
    )(raw, tab, resp)
    first_target, aperture_first, look_start, keep = lax.optimization_barrier(
        (first_target, aperture_first, look_start, keep)
    )
    got = shift(send, [(s * NBLK + t, (1 - s) * NBLK + t) for s in range(2) for t in range(NBLK)])
    own, mine, onward = pl.pallas_call(
        mix_kernel,
        out_shape=[
            jax.ShapeDtypeStruct((WIN, SAMP), F32),
            jax.ShapeDtypeStruct((208, SAMP), BF),
            jax.ShapeDtypeStruct((80, SAMP), BF),
        ],
        in_specs=[sm] * 2 + [vm] * 2,
        out_specs=[vm] * 3,
        compiler_params=pltpu.CompilerParams(vmem_limit_bytes=SMALL_VMEM),
        name="mix",
    )(first_target, aperture_first, keep, got)
    swap = both([(t, t ^ 1) for t in range(NBLK)])
    mate = shift(mine, swap)
    moved = shift(
        jnp.concatenate([onward, mate[:128]], 0),
        both([(t, t + 2) for t in range(0, NBLK - 2, 2)] + [(t, t - 2) for t in range(3, NBLK, 2)]),
    )
    across = shift(mine[:EXT], both([(t, t - 4) for t in range(4, NBLK, 2)]))
    swapped = shift(jnp.concatenate([moved[:192], across], 0), swap)
    return pl.pallas_call(
        look_kernel,
        out_shape=jax.ShapeDtypeStruct((4, 128), F32),
        in_specs=[vm] * 6,
        out_specs=vm,
        compiler_params=pltpu.CompilerParams(vmem_limit_bytes=SMALL_VMEM),
        name="look",
    )(look_start.reshape(1, 4), own, mine, mate, moved, swapped)


def solution(mesh):
    consts = [jnp.asarray(t) for t in tables()]
    body = functools.partial(per_device, *consts)
    return jax.shard_map(
        body,
        mesh=mesh,
        in_specs=(P(("track", "section"), None), P("track"), P("track"), P("track")),
        out_specs=P("track", "section"),
        check_vma=False,
    )
```

time: 36.8 us -> 26.5 us (0.72)
  waiting for transfers between devices: 12.4 us -> 3.69 us
  local copies, waits for them, and re-layouts: 0.95 us -> 0.02 us
  Pallas kernels: 6.44 us -> 5.61 us
  starting transfers between devices: 15.1 us -> 15.5 us
    ppermute x6 -> x5, waiting for transfers between devices: 12.4 us -> 3.69 us  [shift(): return lax.ppermute(value, ('section', 'track'), pairs)]
    unnamed x8 -> x2, local copies, waits for them, and re-layouts: 0.93 us -> 0.01 us
    pallas_call x1, Pallas kernels: 1.2 us -> 0.71 us  [per_device(): pl.pallas_call(look_kernel, out_shape=jax.ShapeDtypeStruct((4, 128), F32)...]
    ppermute x6 -> x5, starting transfers between devices: 15.1 us -> 15.5 us  [shift(): return lax.ppermute(value, ('section', 'track'), pairs)]
  transfers between devices with their start and end apart: 6 -> 5, of which waited for: 3 -> 4; matrix products, arithmetic and copies ran while one was open for 0% -> 0% of each run, Pallas kernels for 0% -> 0%
where the time goes in v2:
time: 26.5 us; the launch traced here: 26.2 us
  starting transfers between devices  15.5 us (58%)
  Pallas kernels  5.61 us (21%)
  waiting for transfers between devices  3.69 us (14%)
  between operations  1.35 us (5%)
    ppermute x5, starting transfers between devices, shift(): return lax.ppermute(value, ('section', 'track'), pairs)  15.5 us
    pallas_call x1, Pallas kernels, per_device(): pl.pallas_call(focus_kernel, out_shape=[jax.ShapeDtypeStruct((ROWS, SAMP)...  4.87 us
    ppermute x5, waiting for transfers between devices, shift(): return lax.ppermute(value, ('section', 'track'), pairs)  3.69 us
    pallas_call x1, Pallas kernels, per_device(): pl.pallas_call(look_kernel, out_shape=jax.ShapeDtypeStruct((4, 128), F32)...  0.71 us
  transfers between devices with their start and end apart: 5, of which 4 were waited for; matrix products, arithmetic and copies ran while one was open for 0% of the time, Pallas kernels for 0%

profile of v2, /device:TPU:7, one launch (start us, length us, event | category | flops | bytes accessed | tf_op | source)
XLA Modules:
  0.0 26.2 jit_solution(4562645727566433940)
XLA Ops:
  0.0 0.0 copy-start
  0.0 4.9 %focus.1 = (bf16[192,256]{1,0:T(8,128)(2,1)S(1)}, f32[192,256]{1,0:T(8,128)S(1)}) custom-call(bf16[192,512]{1,0:T(8,128)(2,1)} %raw_hbm.1, bf16[2624,512]{1,0:T(8,128)(2,1)} %constant.4.clone.tab_hbm, f32[2,13,384,256]{3,2,1,0:T(8,128)} %constant.5.clone.resp_hbm), custom_call_target="tpu_custom_call" | custom-call | tf_op jit(solution)/shard_map/focus/pallas_call | solution.py:251
  4.9 3.0 %collective-permute-start = (bf16[192,256]{1,0:T(8,128)(2,1)S(1)}, bf16[192,256]{1,0:T(8,128)(2,1)S(1)}, u32[]{:S(2)}, u32[]{:S(2)}) collective-permute-start(bf16[192,256]{1,0:T(8,128)(2,1)S(1)} %get-tuple-element.19), channel_id=1, source_target_pairs={{0,64},{1,65},{2,66},{3,67},{4,68},{5,69},{6,70},{7,71},{8,72},{9,... | collective-permute-start | bytes 294920 | tf_op jit(solution)/shard_map/ppermute | solution.py:240
  9.2 0.7 %collective-permute-done.got = bf16[192,256]{1,0:T(8,128)(2,1)S(1)} collective-permute-done((bf16[192,256]{1,0:T(8,128)(2,1)S(1)}, bf16[192,256]{1,0:T(8,128)(2,1)S(1)}, u32[]{:S(2)}, u32[]{:S(2)}) %collective-permute-start) | collective-permute-done | bytes 98336 | tf_op jit(solution)/shard_map/ppermute | solution.py:240
  10.0 1.9 %collective-permute-start.1 = (bf16[208,256]{1,0:T(8,128)(2,1)S(1)}, bf16[208,256]{1,0:T(8,128)(2,1)S(1)}, u32[]{:S(2)}, u32[]{:S(2)}) collective-permute-start(bf16[208,256]{1,0:T(8,128)(2,1)S(1)} %get-tuple-element.21.mine), channel_id=1, source_target_pairs={{0,1},{1,0},{2,3},{3,2},{4,5},{5,4},{6,7},{7,6},{8,9},{9,8},{10,11... | collective-permute-start | bytes 319496 | tf_op jit(solution)/shard_map/ppermute | solution.py:240
  11.9 1.0 %collective-permute-done.1.mate = bf16[208,256]{1,0:T(8,128)(2,1)S(1)} collective-permute-done((bf16[208,256]{1,0:T(8,128)(2,1)S(1)}, bf16[208,256]{1,0:T(8,128)(2,1)S(1)}, u32[]{:S(2)}, u32[]{:S(2)}) %collective-permute-start.1) | collective-permute-done | bytes 106528 | tf_op jit(solution)/shard_map/ppermute | solution.py:240
  12.8 6.9 %collective-permute-start.2 = (bf16[208,256]{1,0:T(8,128)(2,1)S(1)}, bf16[208,256]{1,0:T(8,128)(2,1)S(1)}, u32[]{:S(2)}, u32[]{:S(2)}) collective-permute-start(bf16[208,256]{1,0:T(8,128)(2,1)S(1)} %pad_maximum_fusion.1), channel_id=1, source_target_pairs={{0,2},{2,4},{4,6},{6,8},{8,10},{10,12},{12,14},{14,16},{16,18},{18... | collective-permute-start | bytes 319496 | tf_op jit(solution)/shard_map/ppermute | solution.py:240
  19.8 0.7 %collective-permute-start.3 = (bf16[48,256]{1,0:T(8,128)(2,1)S(1)}, bf16[48,256]{1,0:T(8,128)(2,1)S(1)}, u32[]{:S(2)}, u32[]{:S(2)}) collective-permute-start(bf16[48,256]{1,0:T(8,128)(2,1)S(1)} %slice.11), channel_id=1, source_target_pairs={{4,0},{6,2},{8,4},{10,6},{12,8},{14,10},{16,12},{18,14},{20,16},{2... | collective-permute-start | bytes 73736 | tf_op jit(solution)/shard_map/ppermute | solution.py:240
  20.5 1.0 %collective-permute-done.2.moved = bf16[208,256]{1,0:T(8,128)(2,1)S(1)} collective-permute-done((bf16[208,256]{1,0:T(8,128)(2,1)S(1)}, bf16[208,256]{1,0:T(8,128)(2,1)S(1)}, u32[]{:S(2)}, u32[]{:S(2)}) %collective-permute-start.2) | collective-permute-done | bytes 106528 | tf_op jit(solution)/shard_map/ppermute | solution.py:240
  21.5 0.0 collective-permute-done.3
  21.5 3.0 %collective-permute-start.4 = (bf16[240,256]{1,0:T(8,128)(2,1)S(1)}, bf16[240,256]{1,0:T(8,128)(2,1)S(1)}, u32[]{:S(2)}, u32[]{:S(2)}) collective-permute-start(bf16[240,256]{1,0:T(8,128)(2,1)S(1)} %pad_maximum_fusion), channel_id=1, source_target_pairs={{0,1},{1,0},{2,3},{3,2},{4,5},{5,4},{6,7},{7,6},{8,9},{9,8},{10,11... | collective-permute-start | bytes 368648 | tf_op jit(solution)/shard_map/ppermute | solution.py:240
  24.5 1.0 %collective-permute-done.4.swapped = bf16[240,256]{1,0:T(8,128)(2,1)S(1)} collective-permute-done((bf16[240,256]{1,0:T(8,128)(2,1)S(1)}, bf16[240,256]{1,0:T(8,128)(2,1)S(1)}, u32[]{:S(2)}, u32[]{:S(2)}) %collective-permute-start.4) | collective-permute-done | bytes 122912 | tf_op jit(solution)/shard_map/ppermute | solution.py:240
  25.5 0.0 copy-done
  25.5 0.7 %look.1 = f32[4,128]{1,0:T(4,128)} custom-call(s32[1,4]{1,0:T(1,128)S(1)} %bitcast.1, f32[80,256]{1,0:T(8,128)S(1)} %get-tuple-element.20.own, bf16[208,256]{1,0:T(8,128)(2,1)S(1)} %get-tuple-element.21.mine, bf16[208,256]{1,0:T(8,128)(2,1)S(1)} %collective-permute-done.1.mate, bf16[208,256]{1,0:T(8,128)(2,1)S(1)} %collective-permute-done.2.moved, ...), custom_call_target="tpu_custom_call" | custom-call | tf_op jit(solution)/shard_map/look/pallas_call | solution.py:299
  (6 shorter events, 0.1 us)
Async XLA Ops:
  0.0 25.5 %copy-start = (s32[4]{0:T(128)S(1)}, s32[4]{0:T(128)}, u32[]{:S(2)}) copy-start(s32[4]{0:T(128)} %param.9) | copy-start | bytes 52
  4.9 5.1 %collective-permute-start = (bf16[192,256]{1,0:T(8,128)(2,1)S(1)}, bf16[192,256]{1,0:T(8,128)(2,1)S(1)}, u32[]{:S(2)}, u32[]{:S(2)}) collective-permute-start(bf16[192,256]{1,0:T(8,128)(2,1)S(1)} %get-tuple-element.19), channel_id=1, source_target_pairs={{0,64},{1,65},{2,66},{3,67},{4,68},{5,69},{6,70},{7,71},{8,72},{9,... | collective-permute-start | bytes 294920 | tf_op jit(solution)/shard_map/ppermute | solution.py:240
  10.0 2.9 %collective-permute-start.1 = (bf16[208,256]{1,0:T(8,128)(2,1)S(1)}, bf16[208,256]{1,0:T(8,128)(2,1)S(1)}, u32[]{:S(2)}, u32[]{:S(2)}) collective-permute-start(bf16[208,256]{1,0:T(8,128)(2,1)S(1)} %get-tuple-element.21.mine), channel_id=1, source_target_pairs={{0,1},{1,0},{2,3},{3,2},{4,5},{5,4},{6,7},{7,6},{8,9},{9,8},{10,11... | collective-permute-start | bytes 319496 | tf_op jit(solution)/shard_map/ppermute | solution.py:240
  12.8 8.6 %collective-permute-start.2 = (bf16[208,256]{1,0:T(8,128)(2,1)S(1)}, bf16[208,256]{1,0:T(8,128)(2,1)S(1)}, u32[]{:S(2)}, u32[]{:S(2)}) collective-permute-start(bf16[208,256]{1,0:T(8,128)(2,1)S(1)} %pad_maximum_fusion.1), channel_id=1, source_target_pairs={{0,2},{2,4},{4,6},{6,8},{8,10},{10,12},{12,14},{14,16},{16,18},{18... | collective-permute-start | bytes 319496 | tf_op jit(solution)/shard_map/ppermute | solution.py:240
  19.8 1.7 %collective-permute-start.3 = (bf16[48,256]{1,0:T(8,128)(2,1)S(1)}, bf16[48,256]{1,0:T(8,128)(2,1)S(1)}, u32[]{:S(2)}, u32[]{:S(2)}) collective-permute-start(bf16[48,256]{1,0:T(8,128)(2,1)S(1)} %slice.11), channel_id=1, source_target_pairs={{4,0},{6,2},{8,4},{10,6},{12,8},{14,10},{16,12},{18,14},{20,16},{2... | collective-permute-start | bytes 73736 | tf_op jit(solution)/shard_map/ppermute | solution.py:240
  21.5 4.0 %collective-permute-start.4 = (bf16[240,256]{1,0:T(8,128)(2,1)S(1)}, bf16[240,256]{1,0:T(8,128)(2,1)S(1)}, u32[]{:S(2)}, u32[]{:S(2)}) collective-permute-start(bf16[240,256]{1,0:T(8,128)(2,1)S(1)} %pad_maximum_fusion), channel_id=1, source_target_pairs={{0,1},{1,0},{2,3},{3,2},{4,5},{5,4},{6,7},{7,6},{8,9},{9,8},{10,11... | collective-permute-start | bytes 368648 | tf_op jit(solution)/shard_map/ppermute | solution.py:240

commit v3 on v2

--- a/solution.py
+++ b/solution.py
@@ -18,14 +18,17 @@
 HALF = ECH_DEV // 2
 SUB = HALF // STEP
 ROWS = 192
-NFFT = 208
+WINDOWS = 2
+WROWS = ROWS // WINDOWS
+NFFT = WROWS + SUB
 CHUNK = 16
+CHUNKS = WINDOWS * NFFT // CHUNK
 WIN = 80
 EXT = 48
 VGRP = 4
 FWD_AT = 512
 INV_AT = FWD_AT + VGRP * NFFT
-RANGE_AT = INV_AT + 4 * ROWS
+RANGE_AT = INV_AT + 2 * WROWS
 TAB_END = RANGE_AT + 512
 FOCUS_VMEM = 54912 * 1024
 SMALL_VMEM = 8 * 1024 * 1024
@@ -64,27 +67,27 @@
     kappa = 568.6 + (f - SAMP // 2) * 13.4 / SAMP
     resp = []
     for sec in range(2):
-        j = sec * SUB - 127 + np.arange(NFFT)
-        dist = (STEP * j[None, :] + np.arange(STEP)[:, None]) * (1200.0 / ECH_DEV)
-        delay = dist * dist / (np.sqrt(1.3e6 * 1.3e6 + dist * dist) + 1.3e6)
-        h = np.exp(-1j * delay[:, :, None] * kappa)
-        h = np.roll(h, (sec * SUB - 127) % NFFT, axis=1)
-        spec = np.fft.ifft(h, axis=1)
-        shift = np.exp(-2j * math.pi * ((w * (SUB * sec + 64)) % NFFT) / NFFT)
-        spec = spec * shift[None, :, None] / math.sqrt(4 * ECH_DEV)
-        parts = np.stack([spec.real, spec.imag], 1)
-        parts = parts.reshape(STEP, 2, NFFT // CHUNK, CHUNK, SAMP)
-        resp.append(parts.transpose(2, 0, 1, 3, 4).reshape(NFFT // CHUNK, STEP * 2 * CHUNK, SAMP))
-    resp = np.stack(resp).astype(np.float32)
-
-    r = np.arange(ROWS)
+        for win in range(WINDOWS):
+            m = np.arange(-WROWS, SUB)
+            j = sec * SUB + 64 - win * WROWS + m
+            dist = (STEP * j[None, :] + np.arange(STEP)[:, None]) * (1200.0 / ECH_DEV)
+            delay = dist * dist / (np.sqrt(1.3e6 * 1.3e6 + dist * dist) + 1.3e6)
+            h = np.exp(-1j * delay[:, :, None] * kappa)
+            h = np.roll(h, -WROWS, axis=1)
+            spec = np.fft.ifft(h, axis=1) / math.sqrt(4 * ECH_DEV)
+            parts = np.stack([spec.real, spec.imag], 1)
+            parts = parts.reshape(STEP, 2, NFFT // CHUNK, CHUNK, SAMP)
+            resp.append(parts.transpose(2, 0, 1, 3, 4).reshape(NFFT // CHUNK, STEP * 2 * CHUNK, SAMP))
+    resp = np.stack(resp).astype(np.float32).reshape(2, CHUNKS, STEP * 2 * CHUNK, SAMP)
+
+    r = np.arange(WROWS)
     inv = np.exp(2j * math.pi * (np.outer(r, w) % NFFT) / NFFT)
     inv = np.block([[inv.real, -inv.imag], [inv.imag, inv.real]])
-    inv_table = split_bf16(inv)
+    inv_table = np.zeros((2 * WROWS, 2, SAMP), jnp.bfloat16)
+    inv_table[:, :, : 2 * NFFT] = split_bf16(inv).transpose(1, 0, 2)
 
     base = np.exp(2j * math.pi * turns / SAMP) / math.sqrt(SAMP)
     range_table = split_bf16(np.concatenate([base.real, base.imag], 1))
-    inv_table = np.concatenate([inv_table, np.zeros((2, 2 * ROWS, 512 - 2 * NFFT), inv_table.dtype)], 2)
     fwd_table = np.concatenate([fwd_table[: VGRP * NFFT], fwd_table[VGRP * NFFT :]], 1)
     packed = [comp, fwd_table, inv_table, range_table]
     return np.concatenate([t.reshape(-1, 512) for t in packed], 0), resp
@@ -118,10 +121,11 @@
     raw, comp_t, fwd_t, resp, inv_t, range_t, comp, rhs, spec, img, sems,
 ):
     section = lax.axis_index("section")
-    chunks = NFFT // CHUNK
+    chunks = CHUNKS
     pairs = [(raw_hbm, raw), (tab_hbm.at[:FWD_AT], comp_t), (tab_hbm.at[FWD_AT:INV_AT], fwd_t)]
     pairs += [(resp_hbm.at[section, i], resp.at[i]) for i in range(chunks)]
     pairs += [(tab_hbm.at[INV_AT:RANGE_AT], inv_t), (tab_hbm.at[RANGE_AT:TAB_END], range_t)]
+    pairs = pairs[:3] + pairs[-2:] + pairs[3:-2]
     copies = [pltpu.make_async_copy(src, dst, sems.at[i]) for i, (src, dst) in enumerate(pairs)]
     for copy in copies:
         copy.start()
@@ -143,13 +147,19 @@
     for q in range(STEP // VGRP):
         for n in range(2):
             spec[q, n * VGRP * NFFT : (n + 1) * VGRP * NFFT] = dot(fwd_t[:, n * SAMP : (n + 1) * SAMP], rhs[q])
+    copies[3].wait()
+    copies[4].wait()
+    inv_hi = inv_t[:, : 2 * NFFT]
+    inv_lo = inv_t[:, SAMP : SAMP + 2 * NFFT]
+    image = []
     for i in range(chunks):
-        copies[3 + i].wait()
+        win, j = divmod(i, NFFT // CHUNK)
+        copies[5 + i].wait()
         sum_re = jnp.zeros((CHUNK, SAMP), F32)
         sum_im = jnp.zeros((CHUNK, SAMP), F32)
         for v in range(STEP):
             q, k = divmod(v, VGRP)
-            at = k * 2 * NFFT + i * CHUNK
+            at = k * 2 * NFFT + j * CHUNK
             y_re = spec[q, at : at + CHUNK, :]
             y_im = spec[q, at + NFFT : at + NFFT + CHUNK, :]
             h_re = resp[i, v * 2 * CHUNK : v * 2 * CHUNK + CHUNK, :]
@@ -157,16 +167,13 @@
             sum_re += y_re * h_re - y_im * h_im
             sum_im += y_re * h_im + y_im * h_re
         for n, total in enumerate((sum_re, sum_im)):
-            hi = total.astype(BF)
-            at = n * NFFT + i * CHUNK
-            img[0, at : at + CHUNK, :] = hi
-            img[1, at : at + CHUNK, :] = (total - hi.astype(F32)).astype(BF)
-    copies[3 + chunks].wait()
-    inv_hi = inv_t[: 2 * ROWS, : 2 * NFFT]
-    inv_lo = inv_t[2 * ROWS :, : 2 * NFFT]
-    image = dot(inv_hi, img[0]) + (dot(inv_lo, img[0]) + dot(inv_hi, img[1]))
-    copies[4 + chunks].wait()
-    field_re, field_im = complex_dot([hi_lo(image[:ROWS]), hi_lo(image[ROWS:])], range_t[...])
+            at = n * NFFT + j * CHUNK
+            img[win, 0, at : at + CHUNK, :], img[win, 1, at : at + CHUNK, :] = hi_lo(total)
+        if j == NFFT // CHUNK - 1:
+            image.append(dot(inv_hi, img[win, 0]) + (dot(inv_lo, img[win, 0]) + dot(inv_hi, img[win, 1])))
+    image_re = jnp.concatenate([part[:WROWS] for part in image], 0)
+    image_im = jnp.concatenate([part[WROWS:] for part in image], 0)
+    field_re, field_im = complex_dot([hi_lo(image_re), hi_lo(image_im)], range_t[...])
     low = jnp.concatenate([field_re[:, :128], field_im[:, :128]], 1)
     high = jnp.concatenate([field_re[:, 128:], field_im[:, 128:]], 1)
 
@@ -260,14 +267,14 @@
             pltpu.VMEM((HALF, 512), BF),
             pltpu.VMEM((FWD_AT, 512), BF),
             pltpu.VMEM((VGRP * NFFT, 512), BF),
-            pltpu.VMEM((NFFT // CHUNK, STEP * 2 * CHUNK, SAMP), F32),
-            pltpu.VMEM((4 * ROWS, 512), BF),
+            pltpu.VMEM((CHUNKS, STEP * 2 * CHUNK, SAMP), F32),
+            pltpu.VMEM((2 * WROWS, 512), BF),
             pltpu.VMEM((512, 512), BF),
             pltpu.VMEM((4, HALF, 128), F32),
             pltpu.VMEM((STEP // VGRP, 256, SAMP), BF),
             pltpu.VMEM((STEP // VGRP, VGRP * 2 * NFFT, SAMP), F32),
-            pltpu.VMEM((2, 2 * NFFT, SAMP), BF),
-            pltpu.SemaphoreType.DMA((NFFT // CHUNK + 5,)),
+            pltpu.VMEM((WINDOWS, 2, 2 * NFFT, SAMP), BF),
+            pltpu.SemaphoreType.DMA((CHUNKS + 5,)),
         ],
         compiler_params=pltpu.CompilerParams(vmem_limit_bytes=FOCUS_VMEM),
         name="focus",

time: 26.5 us -> 25.7 us (0.970)
  Pallas kernels: 5.61 us -> 4.81 us
    pallas_call x1, Pallas kernels: 4.87 us -> 4.06 us  [per_device(): pl.pallas_call(focus_kernel, out_shape=[jax.ShapeDtypeStruct((ROWS, SAMP)...]
where the time goes in v3:
time: 25.7 us; the launch traced here: 25.4 us
  starting transfers between devices  15.5 us (60%)
  Pallas kernels  4.81 us (19%)
  waiting for transfers between devices  3.69 us (14%)
  between operations  1.35 us (5%)
    ppermute x5, starting transfers between devices, shift(): return lax.ppermute(value, ('section', 'track'), pairs)  15.5 us
    pallas_call x1, Pallas kernels, per_device(): pl.pallas_call(focus_kernel, out_shape=[jax.ShapeDtypeStruct((ROWS, SAMP)...  4.06 us
    ppermute x5, waiting for transfers between devices, shift(): return lax.ppermute(value, ('section', 'track'), pairs)  3.69 us
    pallas_call x1, Pallas kernels, per_device(): pl.pallas_call(look_kernel, out_shape=jax.ShapeDtypeStruct((4, 128), F32)...  0.71 us
  transfers between devices with their start and end apart: 5, of which 4 were waited for; matrix products, arithmetic and copies ran while one was open for 0% of the time, Pallas kernels for 0%

profile of v3, /device:TPU:7, one launch (start us, length us, event | category | flops | bytes accessed | tf_op | source)
XLA Modules:
  0.0 25.4 jit_solution(5833477893412767830)
XLA Ops:
  0.0 0.0 copy-start
  0.0 4.1 %focus.1 = (bf16[192,256]{1,0:T(8,128)(2,1)S(1)}, f32[192,256]{1,0:T(8,128)S(1)}) custom-call(bf16[192,512]{1,0:T(8,128)(2,1)} %raw_hbm.1, bf16[1664,512]{1,0:T(8,128)(2,1)} %constant.4.clone.tab_hbm, f32[2,14,384,256]{3,2,1,0:T(8,128)} %constant.5.clone.resp_hbm), custom_call_target="tpu_custom_call" | custom-call | tf_op jit(solution)/shard_map/focus/pallas_call | solution.py:258
  4.1 3.0 %collective-permute-start = (bf16[192,256]{1,0:T(8,128)(2,1)S(1)}, bf16[192,256]{1,0:T(8,128)(2,1)S(1)}, u32[]{:S(2)}, u32[]{:S(2)}) collective-permute-start(bf16[192,256]{1,0:T(8,128)(2,1)S(1)} %get-tuple-element.19), channel_id=1, source_target_pairs={{0,64},{1,65},{2,66},{3,67},{4,68},{5,69},{6,70},{7,71},{8,72},{9,... | collective-permute-start | bytes 294920 | tf_op jit(solution)/shard_map/ppermute | solution.py:247
  8.4 0.7 %collective-permute-done.got = bf16[192,256]{1,0:T(8,128)(2,1)S(1)} collective-permute-done((bf16[192,256]{1,0:T(8,128)(2,1)S(1)}, bf16[192,256]{1,0:T(8,128)(2,1)S(1)}, u32[]{:S(2)}, u32[]{:S(2)}) %collective-permute-start) | collective-permute-done | bytes 98336 | tf_op jit(solution)/shard_map/ppermute | solution.py:247
  9.2 1.9 %collective-permute-start.1 = (bf16[208,256]{1,0:T(8,128)(2,1)S(1)}, bf16[208,256]{1,0:T(8,128)(2,1)S(1)}, u32[]{:S(2)}, u32[]{:S(2)}) collective-permute-start(bf16[208,256]{1,0:T(8,128)(2,1)S(1)} %get-tuple-element.21.mine), channel_id=1, source_target_pairs={{0,1},{1,0},{2,3},{3,2},{4,5},{5,4},{6,7},{7,6},{8,9},{9,8},{10,11... | collective-permute-start | bytes 319496 | tf_op jit(solution)/shard_map/ppermute | solution.py:247
  11.1 1.0 %collective-permute-done.1.mate = bf16[208,256]{1,0:T(8,128)(2,1)S(1)} collective-permute-done((bf16[208,256]{1,0:T(8,128)(2,1)S(1)}, bf16[208,256]{1,0:T(8,128)(2,1)S(1)}, u32[]{:S(2)}, u32[]{:S(2)}) %collective-permute-start.1) | collective-permute-done | bytes 106528 | tf_op jit(solution)/shard_map/ppermute | solution.py:247
  12.0 6.9 %collective-permute-start.2 = (bf16[208,256]{1,0:T(8,128)(2,1)S(1)}, bf16[208,256]{1,0:T(8,128)(2,1)S(1)}, u32[]{:S(2)}, u32[]{:S(2)}) collective-permute-start(bf16[208,256]{1,0:T(8,128)(2,1)S(1)} %pad_maximum_fusion.1), channel_id=1, source_target_pairs={{0,2},{2,4},{4,6},{6,8},{8,10},{10,12},{12,14},{14,16},{16,18},{18... | collective-permute-start | bytes 319496 | tf_op jit(solution)/shard_map/ppermute | solution.py:247
  19.0 0.7 %collective-permute-start.3 = (bf16[48,256]{1,0:T(8,128)(2,1)S(1)}, bf16[48,256]{1,0:T(8,128)(2,1)S(1)}, u32[]{:S(2)}, u32[]{:S(2)}) collective-permute-start(bf16[48,256]{1,0:T(8,128)(2,1)S(1)} %slice.11), channel_id=1, source_target_pairs={{4,0},{6,2},{8,4},{10,6},{12,8},{14,10},{16,12},{18,14},{20,16},{2... | collective-permute-start | bytes 73736 | tf_op jit(solution)/shard_map/ppermute | solution.py:247
  19.7 1.0 %collective-permute-done.2.moved = bf16[208,256]{1,0:T(8,128)(2,1)S(1)} collective-permute-done((bf16[208,256]{1,0:T(8,128)(2,1)S(1)}, bf16[208,256]{1,0:T(8,128)(2,1)S(1)}, u32[]{:S(2)}, u32[]{:S(2)}) %collective-permute-start.2) | collective-permute-done | bytes 106528 | tf_op jit(solution)/shard_map/ppermute | solution.py:247
  20.7 0.0 collective-permute-done.3
  20.7 3.0 %collective-permute-start.4 = (bf16[240,256]{1,0:T(8,128)(2,1)S(1)}, bf16[240,256]{1,0:T(8,128)(2,1)S(1)}, u32[]{:S(2)}, u32[]{:S(2)}) collective-permute-start(bf16[240,256]{1,0:T(8,128)(2,1)S(1)} %pad_maximum_fusion), channel_id=1, source_target_pairs={{0,1},{1,0},{2,3},{3,2},{4,5},{5,4},{6,7},{7,6},{8,9},{9,8},{10,11... | collective-permute-start | bytes 368648 | tf_op jit(solution)/shard_map/ppermute | solution.py:247
  23.7 1.0 %collective-permute-done.4.swapped = bf16[240,256]{1,0:T(8,128)(2,1)S(1)} collective-permute-done((bf16[240,256]{1,0:T(8,128)(2,1)S(1)}, bf16[240,256]{1,0:T(8,128)(2,1)S(1)}, u32[]{:S(2)}, u32[]{:S(2)}) %collective-permute-start.4) | collective-permute-done | bytes 122912 | tf_op jit(solution)/shard_map/ppermute | solution.py:247
  24.7 0.0 copy-done
  24.7 0.7 %look.1 = f32[4,128]{1,0:T(4,128)} custom-call(s32[1,4]{1,0:T(1,128)S(1)} %bitcast.1, f32[80,256]{1,0:T(8,128)S(1)} %get-tuple-element.20.own, bf16[208,256]{1,0:T(8,128)(2,1)S(1)} %get-tuple-element.21.mine, bf16[208,256]{1,0:T(8,128)(2,1)S(1)} %collective-permute-done.1.mate, bf16[208,256]{1,0:T(8,128)(2,1)S(1)} %collective-permute-done.2.moved, ...), custom_call_target="tpu_custom_call" | custom-call | tf_op jit(solution)/shard_map/look/pallas_call | solution.py:306
  (6 shorter events, 0.1 us)
Async XLA Ops:
  0.0 24.7 %copy-start = (s32[4]{0:T(128)S(1)}, s32[4]{0:T(128)}, u32[]{:S(2)}) copy-start(s32[4]{0:T(128)} %param.9) | copy-start | bytes 52
  4.1 5.1 %collective-permute-start = (bf16[192,256]{1,0:T(8,128)(2,1)S(1)}, bf16[192,256]{1,0:T(8,128)(2,1)S(1)}, u32[]{:S(2)}, u32[]{:S(2)}) collective-permute-start(bf16[192,256]{1,0:T(8,128)(2,1)S(1)} %get-tuple-element.19), channel_id=1, source_target_pairs={{0,64},{1,65},{2,66},{3,67},{4,68},{5,69},{6,70},{7,71},{8,72},{9,... | collective-permute-start | bytes 294920 | tf_op jit(solution)/shard_map/ppermute | solution.py:247
  9.2 2.9 %collective-permute-start.1 = (bf16[208,256]{1,0:T(8,128)(2,1)S(1)}, bf16[208,256]{1,0:T(8,128)(2,1)S(1)}, u32[]{:S(2)}, u32[]{:S(2)}) collective-permute-start(bf16[208,256]{1,0:T(8,128)(2,1)S(1)} %get-tuple-element.21.mine), channel_id=1, source_target_pairs={{0,1},{1,0},{2,3},{3,2},{4,5},{5,4},{6,7},{7,6},{8,9},{9,8},{10,11... | collective-permute-start | bytes 319496 | tf_op jit(solution)/shard_map/ppermute | solution.py:247
  12.0 8.6 %collective-permute-start.2 = (bf16[208,256]{1,0:T(8,128)(2,1)S(1)}, bf16[208,256]{1,0:T(8,128)(2,1)S(1)}, u32[]{:S(2)}, u32[]{:S(2)}) collective-permute-start(bf16[208,256]{1,0:T(8,128)(2,1)S(1)} %pad_maximum_fusion.1), channel_id=1, source_target_pairs={{0,2},{2,4},{4,6},{6,8},{8,10},{10,12},{12,14},{14,16},{16,18},{18... | collective-permute-start | bytes 319496 | tf_op jit(solution)/shard_map/ppermute | solution.py:247
  19.0 1.7 %collective-permute-start.3 = (bf16[48,256]{1,0:T(8,128)(2,1)S(1)}, bf16[48,256]{1,0:T(8,128)(2,1)S(1)}, u32[]{:S(2)}, u32[]{:S(2)}) collective-permute-start(bf16[48,256]{1,0:T(8,128)(2,1)S(1)} %slice.11), channel_id=1, source_target_pairs={{4,0},{6,2},{8,4},{10,6},{12,8},{14,10},{16,12},{18,14},{20,16},{2... | collective-permute-start | bytes 73736 | tf_op jit(solution)/shard_map/ppermute | solution.py:247
  20.7 4.0 %collective-permute-start.4 = (bf16[240,256]{1,0:T(8,128)(2,1)S(1)}, bf16[240,256]{1,0:T(8,128)(2,1)S(1)}, u32[]{:S(2)}, u32[]{:S(2)}) collective-permute-start(bf16[240,256]{1,0:T(8,128)(2,1)S(1)} %pad_maximum_fusion), channel_id=1, source_target_pairs={{0,1},{1,0},{2,3},{3,2},{4,5},{5,4},{6,7},{7,6},{8,9},{9,8},{10,11... | collective-permute-start | bytes 368648 | tf_op jit(solution)/shard_map/ppermute | solution.py:247

commit v4 on v3

--- a/solution.py
+++ b/solution.py
@@ -26,6 +26,7 @@
 WIN = 80
 EXT = 48
 VGRP = 4
+TOP_CHIPS = 8
 FWD_AT = 512
 INV_AT = FWD_AT + VGRP * NFFT
 RANGE_AT = INV_AT + 2 * WROWS
@@ -301,7 +302,12 @@
         jnp.concatenate([onward, mate[:128]], 0),
         both([(t, t + 2) for t in range(0, NBLK - 2, 2)] + [(t, t - 2) for t in range(3, NBLK, 2)]),
     )
-    across = shift(mine[:EXT], both([(t, t - 4) for t in range(4, NBLK, 2)]))
+    pairs = []
+    for chip in range(2, NBLK // 2):
+        at_bottom = chip % TOP_CHIPS < 2
+        pairs.append((2 * chip + at_bottom, 2 * chip - 4))
+    odd = lax.axis_index("track") % 2 == 1
+    across = shift(jnp.where(odd, mate[:EXT], mine[:EXT]), both(pairs))
     swapped = shift(jnp.concatenate([moved[:192], across], 0), swap)
     return pl.pallas_call(
         look_kernel,

time: 25.7 us -> 25.1 us (0.977)
  starting transfers between devices: 15.5 us -> 14.7 us
    ppermute x5, starting transfers between devices: 15.5 us -> 14.7 us  [shift(): return lax.ppermute(value, ('section', 'track'), pairs)]
where the time goes in v4:
time: 25.1 us; the launch traced here: 24.8 us
  starting transfers between devices  14.7 us (59%)
  Pallas kernels  4.8 us (19%)
  waiting for transfers between devices  3.92 us (16%)
  between operations  1.37 us (5%)
    ppermute x5, starting transfers between devices, shift(): return lax.ppermute(value, ('section', 'track'), pairs)  14.7 us
    pallas_call x1, Pallas kernels, per_device(): pl.pallas_call(focus_kernel, out_shape=[jax.ShapeDtypeStruct((ROWS, SAMP)...  4.06 us
    ppermute x5, waiting for transfers between devices, shift(): return lax.ppermute(value, ('section', 'track'), pairs)  3.92 us
    pallas_call x1, Pallas kernels, per_device(): pl.pallas_call(look_kernel, out_shape=jax.ShapeDtypeStruct((4, 128), F32)...  0.71 us
  transfers between devices with their start and end apart: 5, of which 4 were waited for; matrix products, arithmetic and copies ran while one was open for 0% of the time, Pallas kernels for 0%

profile of v4, /device:TPU:7, one launch (start us, length us, event | category | flops | bytes accessed | tf_op | source)
XLA Modules:
  0.0 24.8 jit_solution(7625923768349586192)
XLA Ops:
  0.0 0.0 copy-start
  0.0 4.1 %focus.1 = (bf16[192,256]{1,0:T(8,128)(2,1)S(1)}, f32[192,256]{1,0:T(8,128)S(1)}) custom-call(bf16[192,512]{1,0:T(8,128)(2,1)} %raw_hbm.1, bf16[1664,512]{1,0:T(8,128)(2,1)} %constant.22.clone.tab_hbm, f32[2,14,384,256]{3,2,1,0:T(8,128)} %constant.23.clone.resp_hbm), custom_call_target="tpu_custom_call" | custom-call | tf_op jit(solution)/shard_map/focus/pallas_call | solution.py:259
  4.1 3.0 %collective-permute-start = (bf16[192,256]{1,0:T(8,128)(2,1)S(1)}, bf16[192,256]{1,0:T(8,128)(2,1)S(1)}, u32[]{:S(2)}, u32[]{:S(2)}) collective-permute-start(bf16[192,256]{1,0:T(8,128)(2,1)S(1)} %get-tuple-element.19), channel_id=1, source_target_pairs={{0,64},{1,65},{2,66},{3,67},{4,68},{5,69},{6,70},{7,71},{8,72},{9,... | collective-permute-start | bytes 294920 | tf_op jit(solution)/shard_map/ppermute | solution.py:248
  8.4 0.7 %collective-permute-done.got = bf16[192,256]{1,0:T(8,128)(2,1)S(1)} collective-permute-done((bf16[192,256]{1,0:T(8,128)(2,1)S(1)}, bf16[192,256]{1,0:T(8,128)(2,1)S(1)}, u32[]{:S(2)}, u32[]{:S(2)}) %collective-permute-start) | collective-permute-done | bytes 98336 | tf_op jit(solution)/shard_map/ppermute | solution.py:248
  9.2 1.9 %collective-permute-start.1 = (bf16[208,256]{1,0:T(8,128)(2,1)S(1)}, bf16[208,256]{1,0:T(8,128)(2,1)S(1)}, u32[]{:S(2)}, u32[]{:S(2)}) collective-permute-start(bf16[208,256]{1,0:T(8,128)(2,1)S(1)} %get-tuple-element.21.mine), channel_id=1, source_target_pairs={{0,1},{1,0},{2,3},{3,2},{4,5},{5,4},{6,7},{7,6},{8,9},{9,8},{10,11... | collective-permute-start | bytes 319496 | tf_op jit(solution)/shard_map/ppermute | solution.py:248
  11.1 1.0 %collective-permute-done.1.mate = bf16[208,256]{1,0:T(8,128)(2,1)S(1)} collective-permute-done((bf16[208,256]{1,0:T(8,128)(2,1)S(1)}, bf16[208,256]{1,0:T(8,128)(2,1)S(1)}, u32[]{:S(2)}, u32[]{:S(2)}) %collective-permute-start.1) | collective-permute-done | bytes 106528 | tf_op jit(solution)/shard_map/ppermute | solution.py:248
  12.0 6.9 %collective-permute-start.2 = (bf16[208,256]{1,0:T(8,128)(2,1)S(1)}, bf16[208,256]{1,0:T(8,128)(2,1)S(1)}, u32[]{:S(2)}, u32[]{:S(2)}) collective-permute-start(bf16[208,256]{1,0:T(8,128)(2,1)S(1)} %pad_maximum_fusion.1), channel_id=1, source_target_pairs={{0,2},{2,4},{4,6},{6,8},{8,10},{10,12},{12,14},{14,16},{16,18},{18... | collective-permute-start | bytes 319496 | tf_op jit(solution)/shard_map/ppermute | solution.py:248
  19.0 2.7 %collective-permute-start.3 = (bf16[48,256]{1,0:T(8,128)(2,1)S(1)}, bf16[48,256]{1,0:T(8,128)(2,1)S(1)}, u32[]{:S(2)}, u32[]{:S(2)}) collective-permute-start(bf16[48,256]{1,0:T(8,128)(2,1)S(1)} %slice_select_fusion), channel_id=1, source_target_pairs={{4,0},{6,2},{8,4},{10,6},{12,8},{14,10},{17,12},{19,14},{20,16},{2... | collective-permute-start | bytes 73736 | tf_op jit(solution)/shard_map/ppermute | solution.py:248
  21.7 0.0 collective-permute-done.2.moved
  21.8 0.9 %collective-permute-done.3 = bf16[48,256]{1,0:T(8,128)(2,1)S(1)} collective-permute-done((bf16[48,256]{1,0:T(8,128)(2,1)S(1)}, bf16[48,256]{1,0:T(8,128)(2,1)S(1)}, u32[]{:S(2)}, u32[]{:S(2)}) %collective-permute-start.3) | collective-permute-done | bytes 24608 | tf_op jit(solution)/shard_map/ppermute | solution.py:248
  22.7 0.1 collective-permute-start.4
  22.8 1.3 %collective-permute-done.4.swapped = bf16[240,256]{1,0:T(8,128)(2,1)S(1)} collective-permute-done((bf16[240,256]{1,0:T(8,128)(2,1)S(1)}, bf16[240,256]{1,0:T(8,128)(2,1)S(1)}, u32[]{:S(2)}, u32[]{:S(2)}) %collective-permute-start.4) | collective-permute-done | bytes 122912 | tf_op jit(solution)/shard_map/ppermute | solution.py:248
  24.1 0.0 copy-done
  24.1 0.7 %look.1 = f32[4,128]{1,0:T(4,128)} custom-call(s32[1,4]{1,0:T(1,128)S(1)} %bitcast.1, f32[80,256]{1,0:T(8,128)S(1)} %get-tuple-element.20.own, bf16[208,256]{1,0:T(8,128)(2,1)S(1)} %get-tuple-element.21.mine, bf16[208,256]{1,0:T(8,128)(2,1)S(1)} %collective-permute-done.1.mate, bf16[208,256]{1,0:T(8,128)(2,1)S(1)} %collective-permute-done.2.moved, ...), custom_call_target="tpu_custom_call" | custom-call | tf_op jit(solution)/shard_map/look/pallas_call | solution.py:312
  (6 shorter events, 0.1 us)
Async XLA Ops:
  0.0 24.1 %copy-start = (s32[4]{0:T(128)S(1)}, s32[4]{0:T(128)}, u32[]{:S(2)}) copy-start(s32[4]{0:T(128)} %param.9) | copy-start | bytes 52
  4.1 5.1 %collective-permute-start = (bf16[192,256]{1,0:T(8,128)(2,1)S(1)}, bf16[192,256]{1,0:T(8,128)(2,1)S(1)}, u32[]{:S(2)}, u32[]{:S(2)}) collective-permute-start(bf16[192,256]{1,0:T(8,128)(2,1)S(1)} %get-tuple-element.19), channel_id=1, source_target_pairs={{0,64},{1,65},{2,66},{3,67},{4,68},{5,69},{6,70},{7,71},{8,72},{9,... | collective-permute-start | bytes 294920 | tf_op jit(solution)/shard_map/ppermute | solution.py:248
  9.2 2.9 %collective-permute-start.1 = (bf16[208,256]{1,0:T(8,128)(2,1)S(1)}, bf16[208,256]{1,0:T(8,128)(2,1)S(1)}, u32[]{:S(2)}, u32[]{:S(2)}) collective-permute-start(bf16[208,256]{1,0:T(8,128)(2,1)S(1)} %get-tuple-element.21.mine), channel_id=1, source_target_pairs={{0,1},{1,0},{2,3},{3,2},{4,5},{5,4},{6,7},{7,6},{8,9},{9,8},{10,11... | collective-permute-start | bytes 319496 | tf_op jit(solution)/shard_map/ppermute | solution.py:248
  12.0 9.7 %collective-permute-start.2 = (bf16[208,256]{1,0:T(8,128)(2,1)S(1)}, bf16[208,256]{1,0:T(8,128)(2,1)S(1)}, u32[]{:S(2)}, u32[]{:S(2)}) collective-permute-start(bf16[208,256]{1,0:T(8,128)(2,1)S(1)} %pad_maximum_fusion.1), channel_id=1, source_target_pairs={{0,2},{2,4},{4,6},{6,8},{8,10},{10,12},{12,14},{14,16},{16,18},{18... | collective-permute-start | bytes 319496 | tf_op jit(solution)/shard_map/ppermute | solution.py:248
  19.0 3.6 %collective-permute-start.3 = (bf16[48,256]{1,0:T(8,128)(2,1)S(1)}, bf16[48,256]{1,0:T(8,128)(2,1)S(1)}, u32[]{:S(2)}, u32[]{:S(2)}) collective-permute-start(bf16[48,256]{1,0:T(8,128)(2,1)S(1)} %slice_select_fusion), channel_id=1, source_target_pairs={{4,0},{6,2},{8,4},{10,6},{12,8},{14,10},{17,12},{19,14},{20,16},{2... | collective-permute-start | bytes 73736 | tf_op jit(solution)/shard_map/ppermute | solution.py:248
  22.7 1.4 %collective-permute-start.4 = (bf16[240,256]{1,0:T(8,128)(2,1)S(1)}, bf16[240,256]{1,0:T(8,128)(2,1)S(1)}, u32[]{:S(2)}, u32[]{:S(2)}) collective-permute-start(bf16[240,256]{1,0:T(8,128)(2,1)S(1)} %pad_maximum_fusion), channel_id=1, source_target_pairs={{0,1},{1,0},{2,3},{3,2},{4,5},{5,4},{6,7},{7,6},{8,9},{9,8},{10,11... | collective-permute-start | bytes 368648 | tf_op jit(solution)/shard_map/ppermute | solution.py:248

commit v5 on v4

--- a/solution.py
+++ b/solution.py
@@ -134,8 +134,8 @@
     copies[1].wait()
     echo_re, echo_im = complex_dot([(raw[:, :SAMP],), (raw[:, SAMP:],)], comp_t[...])
     for n in range(2):
-        comp[n] = echo_re[:, n * 128 : n * 128 + 128]
-        comp[2 + n] = echo_im[:, n * 128 : n * 128 + 128]
+        comp[n, :HALF] = echo_re[:, n * 128 : n * 128 + 128]
+        comp[2 + n, :HALF] = echo_im[:, n * 128 : n * 128 + 128]
     for v in range(STEP):
         rows = [comp[n, pl.ds(v, SUB, stride=STEP), :].astype(BF) for n in range(4)]
         q, i = divmod(v, VGRP)
@@ -271,7 +271,7 @@
             pltpu.VMEM((CHUNKS, STEP * 2 * CHUNK, SAMP), F32),
             pltpu.VMEM((2 * WROWS, 512), BF),
             pltpu.VMEM((512, 512), BF),
-            pltpu.VMEM((4, HALF, 128), F32),
+            pltpu.VMEM((4, HALF + 2 * CHUNK, 128), F32),
             pltpu.VMEM((STEP // VGRP, 256, SAMP), BF),
             pltpu.VMEM((STEP // VGRP, VGRP * 2 * NFFT, SAMP), F32),
             pltpu.VMEM((WINDOWS, 2, 2 * NFFT, SAMP), BF),

time: 25.1 us -> 25.1 us (level)
  no operation moved by 1% of the time
where the time goes in v5:
time: 25.1 us; the launch traced here: 24.8 us
  starting transfers between devices  14.7 us (59%)
  Pallas kernels  4.8 us (19%)
  waiting for transfers between devices  3.92 us (16%)
  between operations  1.37 us (5%)
    ppermute x5, starting transfers between devices, shift(): return lax.ppermute(value, ('section', 'track'), pairs)  14.7 us
    pallas_call x1, Pallas kernels, per_device(): pl.pallas_call(focus_kernel, out_shape=[jax.ShapeDtypeStruct((ROWS, SAMP)...  4.06 us
    ppermute x5, waiting for transfers between devices, shift(): return lax.ppermute(value, ('section', 'track'), pairs)  3.92 us
    pallas_call x1, Pallas kernels, per_device(): pl.pallas_call(look_kernel, out_shape=jax.ShapeDtypeStruct((4, 128), F32)...  0.71 us
  transfers between devices with their start and end apart: 5, of which 4 were waited for; matrix products, arithmetic and copies ran while one was open for 0% of the time, Pallas kernels for 0%

profile of v5, /device:TPU:7, one launch (start us, length us, event | category | flops | bytes accessed | tf_op | source)
XLA Modules:
  0.0 24.8 jit_solution(119671004637268400)
XLA Ops:
  0.0 0.0 copy-start
  0.0 4.1 %focus.1 = (bf16[192,256]{1,0:T(8,128)(2,1)S(1)}, f32[192,256]{1,0:T(8,128)S(1)}) custom-call(bf16[192,512]{1,0:T(8,128)(2,1)} %raw_hbm.1, bf16[1664,512]{1,0:T(8,128)(2,1)} %constant.22.clone.tab_hbm, f32[2,14,384,256]{3,2,1,0:T(8,128)} %constant.23.clone.resp_hbm), custom_call_target="tpu_custom_call" | custom-call | tf_op jit(solution)/shard_map/focus/pallas_call | solution.py:259
  4.1 3.0 %collective-permute-start = (bf16[192,256]{1,0:T(8,128)(2,1)S(1)}, bf16[192,256]{1,0:T(8,128)(2,1)S(1)}, u32[]{:S(2)}, u32[]{:S(2)}) collective-permute-start(bf16[192,256]{1,0:T(8,128)(2,1)S(1)} %get-tuple-element.19), channel_id=1, source_target_pairs={{0,64},{1,65},{2,66},{3,67},{4,68},{5,69},{6,70},{7,71},{8,72},{9,... | collective-permute-start | bytes 294920 | tf_op jit(solution)/shard_map/ppermute | solution.py:248
  8.4 0.7 %collective-permute-done.got = bf16[192,256]{1,0:T(8,128)(2,1)S(1)} collective-permute-done((bf16[192,256]{1,0:T(8,128)(2,1)S(1)}, bf16[192,256]{1,0:T(8,128)(2,1)S(1)}, u32[]{:S(2)}, u32[]{:S(2)}) %collective-permute-start) | collective-permute-done | bytes 98336 | tf_op jit(solution)/shard_map/ppermute | solution.py:248
  9.2 1.9 %collective-permute-start.1 = (bf16[208,256]{1,0:T(8,128)(2,1)S(1)}, bf16[208,256]{1,0:T(8,128)(2,1)S(1)}, u32[]{:S(2)}, u32[]{:S(2)}) collective-permute-start(bf16[208,256]{1,0:T(8,128)(2,1)S(1)} %get-tuple-element.21.mine), channel_id=1, source_target_pairs={{0,1},{1,0},{2,3},{3,2},{4,5},{5,4},{6,7},{7,6},{8,9},{9,8},{10,11... | collective-permute-start | bytes 319496 | tf_op jit(solution)/shard_map/ppermute | solution.py:248
  11.1 1.0 %collective-permute-done.1.mate = bf16[208,256]{1,0:T(8,128)(2,1)S(1)} collective-permute-done((bf16[208,256]{1,0:T(8,128)(2,1)S(1)}, bf16[208,256]{1,0:T(8,128)(2,1)S(1)}, u32[]{:S(2)}, u32[]{:S(2)}) %collective-permute-start.1) | collective-permute-done | bytes 106528 | tf_op jit(solution)/shard_map/ppermute | solution.py:248
  12.0 6.9 %collective-permute-start.2 = (bf16[208,256]{1,0:T(8,128)(2,1)S(1)}, bf16[208,256]{1,0:T(8,128)(2,1)S(1)}, u32[]{:S(2)}, u32[]{:S(2)}) collective-permute-start(bf16[208,256]{1,0:T(8,128)(2,1)S(1)} %pad_maximum_fusion.1), channel_id=1, source_target_pairs={{0,2},{2,4},{4,6},{6,8},{8,10},{10,12},{12,14},{14,16},{16,18},{18... | collective-permute-start | bytes 319496 | tf_op jit(solution)/shard_map/ppermute | solution.py:248
  19.0 2.7 %collective-permute-start.3 = (bf16[48,256]{1,0:T(8,128)(2,1)S(1)}, bf16[48,256]{1,0:T(8,128)(2,1)S(1)}, u32[]{:S(2)}, u32[]{:S(2)}) collective-permute-start(bf16[48,256]{1,0:T(8,128)(2,1)S(1)} %slice_select_fusion), channel_id=1, source_target_pairs={{4,0},{6,2},{8,4},{10,6},{12,8},{14,10},{17,12},{19,14},{20,16},{2... | collective-permute-start | bytes 73736 | tf_op jit(solution)/shard_map/ppermute | solution.py:248
  21.7 0.0 collective-permute-done.2.moved
  21.8 0.9 %collective-permute-done.3 = bf16[48,256]{1,0:T(8,128)(2,1)S(1)} collective-permute-done((bf16[48,256]{1,0:T(8,128)(2,1)S(1)}, bf16[48,256]{1,0:T(8,128)(2,1)S(1)}, u32[]{:S(2)}, u32[]{:S(2)}) %collective-permute-start.3) | collective-permute-done | bytes 24608 | tf_op jit(solution)/shard_map/ppermute | solution.py:248
  22.7 0.1 collective-permute-start.4
  22.8 1.3 %collective-permute-done.4.swapped = bf16[240,256]{1,0:T(8,128)(2,1)S(1)} collective-permute-done((bf16[240,256]{1,0:T(8,128)(2,1)S(1)}, bf16[240,256]{1,0:T(8,128)(2,1)S(1)}, u32[]{:S(2)}, u32[]{:S(2)}) %collective-permute-start.4) | collective-permute-done | bytes 122912 | tf_op jit(solution)/shard_map/ppermute | solution.py:248
  24.1 0.0 copy-done
  24.1 0.7 %look.1 = f32[4,128]{1,0:T(4,128)} custom-call(s32[1,4]{1,0:T(1,128)S(1)} %bitcast.1, f32[80,256]{1,0:T(8,128)S(1)} %get-tuple-element.20.own, bf16[208,256]{1,0:T(8,128)(2,1)S(1)} %get-tuple-element.21.mine, bf16[208,256]{1,0:T(8,128)(2,1)S(1)} %collective-permute-done.1.mate, bf16[208,256]{1,0:T(8,128)(2,1)S(1)} %collective-permute-done.2.moved, ...), custom_call_target="tpu_custom_call" | custom-call | tf_op jit(solution)/shard_map/look/pallas_call | solution.py:312
  (6 shorter events, 0.1 us)
Async XLA Ops:
  0.0 24.1 %copy-start = (s32[4]{0:T(128)S(1)}, s32[4]{0:T(128)}, u32[]{:S(2)}) copy-start(s32[4]{0:T(128)} %param.9) | copy-start | bytes 52
  4.1 5.1 %collective-permute-start = (bf16[192,256]{1,0:T(8,128)(2,1)S(1)}, bf16[192,256]{1,0:T(8,128)(2,1)S(1)}, u32[]{:S(2)}, u32[]{:S(2)}) collective-permute-start(bf16[192,256]{1,0:T(8,128)(2,1)S(1)} %get-tuple-element.19), channel_id=1, source_target_pairs={{0,64},{1,65},{2,66},{3,67},{4,68},{5,69},{6,70},{7,71},{8,72},{9,... | collective-permute-start | bytes 294920 | tf_op jit(solution)/shard_map/ppermute | solution.py:248
  9.2 2.9 %collective-permute-start.1 = (bf16[208,256]{1,0:T(8,128)(2,1)S(1)}, bf16[208,256]{1,0:T(8,128)(2,1)S(1)}, u32[]{:S(2)}, u32[]{:S(2)}) collective-permute-start(bf16[208,256]{1,0:T(8,128)(2,1)S(1)} %get-tuple-element.21.mine), channel_id=1, source_target_pairs={{0,1},{1,0},{2,3},{3,2},{4,5},{5,4},{6,7},{7,6},{8,9},{9,8},{10,11... | collective-permute-start | bytes 319496 | tf_op jit(solution)/shard_map/ppermute | solution.py:248
  12.0 9.7 %collective-permute-start.2 = (bf16[208,256]{1,0:T(8,128)(2,1)S(1)}, bf16[208,256]{1,0:T(8,128)(2,1)S(1)}, u32[]{:S(2)}, u32[]{:S(2)}) collective-permute-start(bf16[208,256]{1,0:T(8,128)(2,1)S(1)} %pad_maximum_fusion.1), channel_id=1, source_target_pairs={{0,2},{2,4},{4,6},{6,8},{8,10},{10,12},{12,14},{14,16},{16,18},{18... | collective-permute-start | bytes 319496 | tf_op jit(solution)/shard_map/ppermute | solution.py:248
  19.0 3.6 %collective-permute-start.3 = (bf16[48,256]{1,0:T(8,128)(2,1)S(1)}, bf16[48,256]{1,0:T(8,128)(2,1)S(1)}, u32[]{:S(2)}, u32[]{:S(2)}) collective-permute-start(bf16[48,256]{1,0:T(8,128)(2,1)S(1)} %slice_select_fusion), channel_id=1, source_target_pairs={{4,0},{6,2},{8,4},{10,6},{12,8},{14,10},{17,12},{19,14},{20,16},{2... | collective-permute-start | bytes 73736 | tf_op jit(solution)/shard_map/ppermute | solution.py:248
  22.7 1.4 %collective-permute-start.4 = (bf16[240,256]{1,0:T(8,128)(2,1)S(1)}, bf16[240,256]{1,0:T(8,128)(2,1)S(1)}, u32[]{:S(2)}, u32[]{:S(2)}) collective-permute-start(bf16[240,256]{1,0:T(8,128)(2,1)S(1)} %pad_maximum_fusion), channel_id=1, source_target_pairs={{0,1},{1,0},{2,3},{3,2},{4,5},{5,4},{6,7},{7,6},{8,9},{9,8},{10,11... | collective-permute-start | bytes 368648 | tf_op jit(solution)/shard_map/ppermute | solution.py:248

commit v6 on v5

--- a/solution.py
+++ b/solution.py
@@ -103,9 +103,10 @@
     re, im = parts
     sums = []
     for part in (re, im):
-        total = dot(part[0], table[:rows]) + dot(part[0], table[rows:])
         if len(part) > 1:
-            total = total + dot(part[1], table[:rows])
+            total = dot(jnp.concatenate([part[0], *part], 1), jnp.concatenate([table, table[:rows]], 0))
+        else:
+            total = dot(jnp.concatenate([part[0], part[0]], 1), table)
         sums.append(total)
     width = table.shape[1] // 2
     return sums[0][:, :width] - sums[1][:, width:], sums[0][:, width:] + sums[1][:, :width]

time: 25.1 us -> 25.1 us (level)
  no operation moved by 1% of the time
where the time goes in v6:
time: 25.1 us; the launch traced here: 24.8 us
  starting transfers between devices  14.7 us (59%)
  Pallas kernels  4.8 us (19%)
  waiting for transfers between devices  3.92 us (16%)
  between operations  1.37 us (5%)
    ppermute x5, starting transfers between devices, shift(): return lax.ppermute(value, ('section', 'track'), pairs)  14.7 us
    pallas_call x1, Pallas kernels, per_device(): pl.pallas_call(focus_kernel, out_shape=[jax.ShapeDtypeStruct((ROWS, SAMP)...  4.06 us
    ppermute x5, waiting for transfers between devices, shift(): return lax.ppermute(value, ('section', 'track'), pairs)  3.92 us
    pallas_call x1, Pallas kernels, per_device(): pl.pallas_call(look_kernel, out_shape=jax.ShapeDtypeStruct((4, 128), F32)...  0.71 us
  transfers between devices with their start and end apart: 5, of which 4 were waited for; matrix products, arithmetic and copies ran while one was open for 0% of the time, Pallas kernels for 0%

profile of v6, /device:TPU:7, one launch (start us, length us, event | category | flops | bytes accessed | tf_op | source)
XLA Modules:
  0.0 24.8 jit_solution(15388053671602773545)
XLA Ops:
  0.0 0.0 copy-start
  0.0 4.1 %focus.1 = (bf16[192,256]{1,0:T(8,128)(2,1)S(1)}, f32[192,256]{1,0:T(8,128)S(1)}) custom-call(bf16[192,512]{1,0:T(8,128)(2,1)} %raw_hbm.1, bf16[1664,512]{1,0:T(8,128)(2,1)} %constant.22.clone.tab_hbm, f32[2,14,384,256]{3,2,1,0:T(8,128)} %constant.23.clone.resp_hbm), custom_call_target="tpu_custom_call" | custom-call | tf_op jit(solution)/shard_map/focus/pallas_call | solution.py:260
  4.1 3.0 %collective-permute-start = (bf16[192,256]{1,0:T(8,128)(2,1)S(1)}, bf16[192,256]{1,0:T(8,128)(2,1)S(1)}, u32[]{:S(2)}, u32[]{:S(2)}) collective-permute-start(bf16[192,256]{1,0:T(8,128)(2,1)S(1)} %get-tuple-element.19), channel_id=1, source_target_pairs={{0,64},{1,65},{2,66},{3,67},{4,68},{5,69},{6,70},{7,71},{8,72},{9,... | collective-permute-start | bytes 294920 | tf_op jit(solution)/shard_map/ppermute | solution.py:249
  8.4 0.7 %collective-permute-done.got = bf16[192,256]{1,0:T(8,128)(2,1)S(1)} collective-permute-done((bf16[192,256]{1,0:T(8,128)(2,1)S(1)}, bf16[192,256]{1,0:T(8,128)(2,1)S(1)}, u32[]{:S(2)}, u32[]{:S(2)}) %collective-permute-start) | collective-permute-done | bytes 98336 | tf_op jit(solution)/shard_map/ppermute | solution.py:249
  9.2 1.9 %collective-permute-start.1 = (bf16[208,256]{1,0:T(8,128)(2,1)S(1)}, bf16[208,256]{1,0:T(8,128)(2,1)S(1)}, u32[]{:S(2)}, u32[]{:S(2)}) collective-permute-start(bf16[208,256]{1,0:T(8,128)(2,1)S(1)} %get-tuple-element.21.mine), channel_id=1, source_target_pairs={{0,1},{1,0},{2,3},{3,2},{4,5},{5,4},{6,7},{7,6},{8,9},{9,8},{10,11... | collective-permute-start | bytes 319496 | tf_op jit(solution)/shard_map/ppermute | solution.py:249
  11.1 1.0 %collective-permute-done.1.mate = bf16[208,256]{1,0:T(8,128)(2,1)S(1)} collective-permute-done((bf16[208,256]{1,0:T(8,128)(2,1)S(1)}, bf16[208,256]{1,0:T(8,128)(2,1)S(1)}, u32[]{:S(2)}, u32[]{:S(2)}) %collective-permute-start.1) | collective-permute-done | bytes 106528 | tf_op jit(solution)/shard_map/ppermute | solution.py:249
  12.0 6.9 %collective-permute-start.2 = (bf16[208,256]{1,0:T(8,128)(2,1)S(1)}, bf16[208,256]{1,0:T(8,128)(2,1)S(1)}, u32[]{:S(2)}, u32[]{:S(2)}) collective-permute-start(bf16[208,256]{1,0:T(8,128)(2,1)S(1)} %pad_maximum_fusion.1), channel_id=1, source_target_pairs={{0,2},{2,4},{4,6},{6,8},{8,10},{10,12},{12,14},{14,16},{16,18},{18... | collective-permute-start | bytes 319496 | tf_op jit(solution)/shard_map/ppermute | solution.py:249
  19.0 2.7 %collective-permute-start.3 = (bf16[48,256]{1,0:T(8,128)(2,1)S(1)}, bf16[48,256]{1,0:T(8,128)(2,1)S(1)}, u32[]{:S(2)}, u32[]{:S(2)}) collective-permute-start(bf16[48,256]{1,0:T(8,128)(2,1)S(1)} %slice_select_fusion), channel_id=1, source_target_pairs={{4,0},{6,2},{8,4},{10,6},{12,8},{14,10},{17,12},{19,14},{20,16},{2... | collective-permute-start | bytes 73736 | tf_op jit(solution)/shard_map/ppermute | solution.py:249
  21.7 0.0 collective-permute-done.2.moved
  21.8 0.9 %collective-permute-done.3 = bf16[48,256]{1,0:T(8,128)(2,1)S(1)} collective-permute-done((bf16[48,256]{1,0:T(8,128)(2,1)S(1)}, bf16[48,256]{1,0:T(8,128)(2,1)S(1)}, u32[]{:S(2)}, u32[]{:S(2)}) %collective-permute-start.3) | collective-permute-done | bytes 24608 | tf_op jit(solution)/shard_map/ppermute | solution.py:249
  22.7 0.1 collective-permute-start.4
  22.8 1.3 %collective-permute-done.4.swapped = bf16[240,256]{1,0:T(8,128)(2,1)S(1)} collective-permute-done((bf16[240,256]{1,0:T(8,128)(2,1)S(1)}, bf16[240,256]{1,0:T(8,128)(2,1)S(1)}, u32[]{:S(2)}, u32[]{:S(2)}) %collective-permute-start.4) | collective-permute-done | bytes 122912 | tf_op jit(solution)/shard_map/ppermute | solution.py:249
  24.1 0.0 copy-done
  24.1 0.7 %look.1 = f32[4,128]{1,0:T(4,128)} custom-call(s32[1,4]{1,0:T(1,128)S(1)} %bitcast.1, f32[80,256]{1,0:T(8,128)S(1)} %get-tuple-element.20.own, bf16[208,256]{1,0:T(8,128)(2,1)S(1)} %get-tuple-element.21.mine, bf16[208,256]{1,0:T(8,128)(2,1)S(1)} %collective-permute-done.1.mate, bf16[208,256]{1,0:T(8,128)(2,1)S(1)} %collective-permute-done.2.moved, ...), custom_call_target="tpu_custom_call" | custom-call | tf_op jit(solution)/shard_map/look/pallas_call | solution.py:313
  (6 shorter events, 0.1 us)
Async XLA Ops:
  0.0 24.1 %copy-start = (s32[4]{0:T(128)S(1)}, s32[4]{0:T(128)}, u32[]{:S(2)}) copy-start(s32[4]{0:T(128)} %param.9) | copy-start | bytes 52
  4.1 5.1 %collective-permute-start = (bf16[192,256]{1,0:T(8,128)(2,1)S(1)}, bf16[192,256]{1,0:T(8,128)(2,1)S(1)}, u32[]{:S(2)}, u32[]{:S(2)}) collective-permute-start(bf16[192,256]{1,0:T(8,128)(2,1)S(1)} %get-tuple-element.19), channel_id=1, source_target_pairs={{0,64},{1,65},{2,66},{3,67},{4,68},{5,69},{6,70},{7,71},{8,72},{9,... | collective-permute-start | bytes 294920 | tf_op jit(solution)/shard_map/ppermute | solution.py:249
  9.2 2.9 %collective-permute-start.1 = (bf16[208,256]{1,0:T(8,128)(2,1)S(1)}, bf16[208,256]{1,0:T(8,128)(2,1)S(1)}, u32[]{:S(2)}, u32[]{:S(2)}) collective-permute-start(bf16[208,256]{1,0:T(8,128)(2,1)S(1)} %get-tuple-element.21.mine), channel_id=1, source_target_pairs={{0,1},{1,0},{2,3},{3,2},{4,5},{5,4},{6,7},{7,6},{8,9},{9,8},{10,11... | collective-permute-start | bytes 319496 | tf_op jit(solution)/shard_map/ppermute | solution.py:249
  12.0 9.7 %collective-permute-start.2 = (bf16[208,256]{1,0:T(8,128)(2,1)S(1)}, bf16[208,256]{1,0:T(8,128)(2,1)S(1)}, u32[]{:S(2)}, u32[]{:S(2)}) collective-permute-start(bf16[208,256]{1,0:T(8,128)(2,1)S(1)} %pad_maximum_fusion.1), channel_id=1, source_target_pairs={{0,2},{2,4},{4,6},{6,8},{8,10},{10,12},{12,14},{14,16},{16,18},{18... | collective-permute-start | bytes 319496 | tf_op jit(solution)/shard_map/ppermute | solution.py:249
  19.0 3.6 %collective-permute-start.3 = (bf16[48,256]{1,0:T(8,128)(2,1)S(1)}, bf16[48,256]{1,0:T(8,128)(2,1)S(1)}, u32[]{:S(2)}, u32[]{:S(2)}) collective-permute-start(bf16[48,256]{1,0:T(8,128)(2,1)S(1)} %slice_select_fusion), channel_id=1, source_target_pairs={{4,0},{6,2},{8,4},{10,6},{12,8},{14,10},{17,12},{19,14},{20,16},{2... | collective-permute-start | bytes 73736 | tf_op jit(solution)/shard_map/ppermute | solution.py:249
  22.7 1.4 %collective-permute-start.4 = (bf16[240,256]{1,0:T(8,128)(2,1)S(1)}, bf16[240,256]{1,0:T(8,128)(2,1)S(1)}, u32[]{:S(2)}, u32[]{:S(2)}) collective-permute-start(bf16[240,256]{1,0:T(8,128)(2,1)S(1)} %pad_maximum_fusion), channel_id=1, source_target_pairs={{0,1},{1,0},{2,3},{3,2},{4,5},{5,4},{6,7},{7,6},{8,9},{9,8},{10,11... | collective-permute-start | bytes 368648 | tf_op jit(solution)/shard_map/ppermute | solution.py:249

commit v7 on v6

--- a/solution.py
+++ b/solution.py
@@ -193,7 +193,7 @@
 def mix_kernel(first_ref, low_ref, keep, got, own, mine, onward):
     block = lax.axis_index("track")
     lane = lax.broadcasted_iota(jnp.int32, (16, SAMP), 1)
-    info = jnp.where(lane < 128, first_ref[0] - block * TB, low_ref[0] - block + 2)
+    info = jnp.where(lane < 128, first_ref[...] - block * TB, low_ref[...] - block + 2)
     field = keep[...] + got[...].astype(F32)
     own[...] = field[64 : 64 + WIN]
     mine[112:128, :] = info.astype(F32).astype(BF)
@@ -292,11 +292,11 @@
             jax.ShapeDtypeStruct((208, SAMP), BF),
             jax.ShapeDtypeStruct((80, SAMP), BF),
         ],
-        in_specs=[sm] * 2 + [vm] * 2,
+        in_specs=[vm] * 4,
         out_specs=[vm] * 3,
         compiler_params=pltpu.CompilerParams(vmem_limit_bytes=SMALL_VMEM),
         name="mix",
-    )(first_target, aperture_first, keep, got)
+    )(first_target.reshape(1, 1), aperture_first.reshape(1, 1), keep, got)
     swap = both([(t, t ^ 1) for t in range(NBLK)])
     mate = shift(mine, swap)
     moved = shift(

time: 25.1 us -> 25.1 us (level)
  no operation moved by 1% of the time
where the time goes in v7:
time: 25.1 us; the launch traced here: 24.8 us
  starting transfers between devices  14.6 us (58%)
  Pallas kernels  4.87 us (19%)
  waiting for transfers between devices  3.92 us (16%)
  between operations  1.37 us (5%)
    ppermute x5, starting transfers between devices, shift(): return lax.ppermute(value, ('section', 'track'), pairs)  14.6 us
    pallas_call x1, Pallas kernels, per_device(): pl.pallas_call(focus_kernel, out_shape=[jax.ShapeDtypeStruct((ROWS, SAMP)...  4.06 us
    ppermute x5, waiting for transfers between devices, shift(): return lax.ppermute(value, ('section', 'track'), pairs)  3.92 us
    pallas_call x1, Pallas kernels, per_device(): pl.pallas_call(look_kernel, out_shape=jax.ShapeDtypeStruct((4, 128), F32)...  0.71 us
  transfers between devices with their start and end apart: 5, of which 4 were waited for; matrix products, arithmetic and copies ran while one was open for 0% of the time, Pallas kernels for 0%

profile of v7, /device:TPU:7, one launch (start us, length us, event | category | flops | bytes accessed | tf_op | source)
XLA Modules:
  0.0 24.8 jit_solution(16692288782346080634)
XLA Ops:
  0.0 0.0 copy-start
  0.0 4.1 %focus.1 = (bf16[192,256]{1,0:T(8,128)(2,1)S(1)}, f32[192,256]{1,0:T(8,128)S(1)}) custom-call(bf16[192,512]{1,0:T(8,128)(2,1)} %raw_hbm.1, bf16[1664,512]{1,0:T(8,128)(2,1)} %constant.22.clone.tab_hbm, f32[2,14,384,256]{3,2,1,0:T(8,128)} %constant.23.clone.resp_hbm), custom_call_target="tpu_custom_call" | custom-call | tf_op jit(solution)/shard_map/focus/pallas_call | solution.py:260
  4.1 3.0 %collective-permute-start = (bf16[192,256]{1,0:T(8,128)(2,1)S(1)}, bf16[192,256]{1,0:T(8,128)(2,1)S(1)}, u32[]{:S(2)}, u32[]{:S(2)}) collective-permute-start(bf16[192,256]{1,0:T(8,128)(2,1)S(1)} %get-tuple-element.19), channel_id=1, source_target_pairs={{0,64},{1,65},{2,66},{3,67},{4,68},{5,69},{6,70},{7,71},{8,72},{9,... | collective-permute-start | bytes 294920 | tf_op jit(solution)/shard_map/ppermute | solution.py:249
  8.4 0.7 %collective-permute-done.got = bf16[192,256]{1,0:T(8,128)(2,1)S(1)} collective-permute-done((bf16[192,256]{1,0:T(8,128)(2,1)S(1)}, bf16[192,256]{1,0:T(8,128)(2,1)S(1)}, u32[]{:S(2)}, u32[]{:S(2)}) %collective-permute-start) | collective-permute-done | bytes 98336 | tf_op jit(solution)/shard_map/ppermute | solution.py:249
  9.1 0.1 mix.1
  9.2 1.9 %collective-permute-start.1 = (bf16[208,256]{1,0:T(8,128)(2,1)S(1)}, bf16[208,256]{1,0:T(8,128)(2,1)S(1)}, u32[]{:S(2)}, u32[]{:S(2)}) collective-permute-start(bf16[208,256]{1,0:T(8,128)(2,1)S(1)} %get-tuple-element.21.mine), channel_id=1, source_target_pairs={{0,1},{1,0},{2,3},{3,2},{4,5},{5,4},{6,7},{7,6},{8,9},{9,8},{10,11... | collective-permute-start | bytes 319496 | tf_op jit(solution)/shard_map/ppermute | solution.py:249
  11.1 1.0 %collective-permute-done.1.mate = bf16[208,256]{1,0:T(8,128)(2,1)S(1)} collective-permute-done((bf16[208,256]{1,0:T(8,128)(2,1)S(1)}, bf16[208,256]{1,0:T(8,128)(2,1)S(1)}, u32[]{:S(2)}, u32[]{:S(2)}) %collective-permute-start.1) | collective-permute-done | bytes 106528 | tf_op jit(solution)/shard_map/ppermute | solution.py:249
  12.1 6.9 %collective-permute-start.2 = (bf16[208,256]{1,0:T(8,128)(2,1)S(1)}, bf16[208,256]{1,0:T(8,128)(2,1)S(1)}, u32[]{:S(2)}, u32[]{:S(2)}) collective-permute-start(bf16[208,256]{1,0:T(8,128)(2,1)S(1)} %pad_maximum_fusion.1), channel_id=1, source_target_pairs={{0,2},{2,4},{4,6},{6,8},{8,10},{10,12},{12,14},{14,16},{16,18},{18... | collective-permute-start | bytes 319496 | tf_op jit(solution)/shard_map/ppermute | solution.py:249
  19.0 2.7 %collective-permute-start.3 = (bf16[48,256]{1,0:T(8,128)(2,1)S(1)}, bf16[48,256]{1,0:T(8,128)(2,1)S(1)}, u32[]{:S(2)}, u32[]{:S(2)}) collective-permute-start(bf16[48,256]{1,0:T(8,128)(2,1)S(1)} %slice_select_fusion), channel_id=1, source_target_pairs={{4,0},{6,2},{8,4},{10,6},{12,8},{14,10},{17,12},{19,14},{20,16},{2... | collective-permute-start | bytes 73736 | tf_op jit(solution)/shard_map/ppermute | solution.py:249
  21.7 0.0 collective-permute-done.2.moved
  21.8 0.9 %collective-permute-done.3 = bf16[48,256]{1,0:T(8,128)(2,1)S(1)} collective-permute-done((bf16[48,256]{1,0:T(8,128)(2,1)S(1)}, bf16[48,256]{1,0:T(8,128)(2,1)S(1)}, u32[]{:S(2)}, u32[]{:S(2)}) %collective-permute-start.3) | collective-permute-done | bytes 24608 | tf_op jit(solution)/shard_map/ppermute | solution.py:249
  22.7 0.1 collective-permute-start.4
  22.8 1.3 %collective-permute-done.4.swapped = bf16[240,256]{1,0:T(8,128)(2,1)S(1)} collective-permute-done((bf16[240,256]{1,0:T(8,128)(2,1)S(1)}, bf16[240,256]{1,0:T(8,128)(2,1)S(1)}, u32[]{:S(2)}, u32[]{:S(2)}) %collective-permute-start.4) | collective-permute-done | bytes 122912 | tf_op jit(solution)/shard_map/ppermute | solution.py:249
  24.1 0.0 copy-done
  24.1 0.7 %look.1 = f32[4,128]{1,0:T(4,128)} custom-call(s32[1,4]{1,0:T(1,128)S(1)} %bitcast.5, f32[80,256]{1,0:T(8,128)S(1)} %get-tuple-element.20.own, bf16[208,256]{1,0:T(8,128)(2,1)S(1)} %get-tuple-element.21.mine, bf16[208,256]{1,0:T(8,128)(2,1)S(1)} %collective-permute-done.1.mate, bf16[208,256]{1,0:T(8,128)(2,1)S(1)} %collective-permute-done.2.moved, ...), custom_call_target="tpu_custom_call" | custom-call | tf_op jit(solution)/shard_map/look/pallas_call | solution.py:313
  (5 shorter events, 0.0 us)
Async XLA Ops:
  0.0 24.1 %copy-start = (s32[4]{0:T(128)S(1)}, s32[4]{0:T(128)}, u32[]{:S(2)}) copy-start(s32[4]{0:T(128)} %param.9) | copy-start | bytes 52
  4.1 5.1 %collective-permute-start = (bf16[192,256]{1,0:T(8,128)(2,1)S(1)}, bf16[192,256]{1,0:T(8,128)(2,1)S(1)}, u32[]{:S(2)}, u32[]{:S(2)}) collective-permute-start(bf16[192,256]{1,0:T(8,128)(2,1)S(1)} %get-tuple-element.19), channel_id=1, source_target_pairs={{0,64},{1,65},{2,66},{3,67},{4,68},{5,69},{6,70},{7,71},{8,72},{9,... | collective-permute-start | bytes 294920 | tf_op jit(solution)/shard_map/ppermute | solution.py:249
  9.2 2.8 %collective-permute-start.1 = (bf16[208,256]{1,0:T(8,128)(2,1)S(1)}, bf16[208,256]{1,0:T(8,128)(2,1)S(1)}, u32[]{:S(2)}, u32[]{:S(2)}) collective-permute-start(bf16[208,256]{1,0:T(8,128)(2,1)S(1)} %get-tuple-element.21.mine), channel_id=1, source_target_pairs={{0,1},{1,0},{2,3},{3,2},{4,5},{5,4},{6,7},{7,6},{8,9},{9,8},{10,11... | collective-permute-start | bytes 319496 | tf_op jit(solution)/shard_map/ppermute | solution.py:249
  12.1 9.7 %collective-permute-start.2 = (bf16[208,256]{1,0:T(8,128)(2,1)S(1)}, bf16[208,256]{1,0:T(8,128)(2,1)S(1)}, u32[]{:S(2)}, u32[]{:S(2)}) collective-permute-start(bf16[208,256]{1,0:T(8,128)(2,1)S(1)} %pad_maximum_fusion.1), channel_id=1, source_target_pairs={{0,2},{2,4},{4,6},{6,8},{8,10},{10,12},{12,14},{14,16},{16,18},{18... | collective-permute-start | bytes 319496 | tf_op jit(solution)/shard_map/ppermute | solution.py:249
  19.0 3.6 %collective-permute-start.3 = (bf16[48,256]{1,0:T(8,128)(2,1)S(1)}, bf16[48,256]{1,0:T(8,128)(2,1)S(1)}, u32[]{:S(2)}, u32[]{:S(2)}) collective-permute-start(bf16[48,256]{1,0:T(8,128)(2,1)S(1)} %slice_select_fusion), channel_id=1, source_target_pairs={{4,0},{6,2},{8,4},{10,6},{12,8},{14,10},{17,12},{19,14},{20,16},{2... | collective-permute-start | bytes 73736 | tf_op jit(solution)/shard_map/ppermute | solution.py:249
  22.7 1.4 %collective-permute-start.4 = (bf16[240,256]{1,0:T(8,128)(2,1)S(1)}, bf16[240,256]{1,0:T(8,128)(2,1)S(1)}, u32[]{:S(2)}, u32[]{:S(2)}) collective-permute-start(bf16[240,256]{1,0:T(8,128)(2,1)S(1)} %pad_maximum_fusion), channel_id=1, source_target_pairs={{0,1},{1,0},{2,3},{3,2},{4,5},{5,4},{6,7},{7,6},{8,9},{9,8},{10,11... | collective-permute-start | bytes 368648 | tf_op jit(solution)/shard_map/ppermute | solution.py:249
